TPU v7x, 32 devices: a whole 2x2x4 slice. The times are simulated.
32 devices in a mesh: lon: 4 (over x, core), lat: 8 (over z, y).
Axes of the slice: x: 2, y: 2, z: 4, core: 2. Of those that a mesh axis runs over, the one named last changes fastest.
Arguments:
- ocean_status: float32 [128, 3, 64, 2048], P(None, None, 'lat', 'lon'), may hold values from -4 to 4
- height_driver: bfloat16 [128, 64, 2048], P(None, 'lat', 'lon'), may hold values from -4 to 4
- obs_index: int32 [8, 4, 64], P('lat', 'lon'), may hold values from 0 to 4095
- obs_value: float32 [8, 4, 64], P('lat', 'lon'), may hold values from -5 to 5
- obs_error: float32 [8, 4, 64], P('lat', 'lon'), may hold values from 1 to 10
Outputs:
- analysis: float32 [128, 3, 64, 2048], P(None, None, 'lat', 'lon')
Inputs may be any that keep to these rules, and one draw needn't show every extreme that they name: `obs_index`: an observation's cell inside its device's tile, the tile's row times 512 plus its column.
All inputs are finite; a program needn't handle non-finite values.
Results may differ from a plain program's by a relative error of at most 0.0003.
Values sent between devices are 32-bit elements; how exact they have to be, the bound alone decides.
A program may use at most 128 MiB of HBM per device.

v0:
```python
import math

import jax
import jax.numpy as jnp
from jax import lax
from jax.sharding import PartitionSpec as P

NS_ITERS = 14


PRECISE = lax.Precision.HIGHEST
GRAVITY = 1.0
DEPTH_MEAN = 1.0
COURANT = 0.2
DIFFUSION = 0.1
FORCE_STEP = 0.5
CORIOLIS_MAX = 0.3


def with_halo(cells, sides, width, closed):
    for axis, dim in sides:
        count = lax.axis_size(axis)
        ends = count if closed else count - 1
        head = lax.slice_in_dim(cells, 0, width, axis=dim)
        tail = lax.slice_in_dim(cells, cells.shape[dim] - width, cells.shape[dim], axis=dim)
        cells = jnp.concatenate(
            [
                lax.ppermute(tail, axis, [(i, (i + 1) % count) for i in range(ends)]),
                cells,
                lax.ppermute(head, axis, [((i + 1) % count, i) for i in range(ends)]),
            ],
            axis=dim,
        )
    return cells


def centre(field):
    return field[..., 1:-1, 1:-1]


def east_of(field):
    return field[..., 1:-1, 2:]


def west_of(field):
    return field[..., 1:-1, :-2]


def north_of(field):
    return field[..., 2:, 1:-1]


def south_of(field):
    return field[..., :-2, 1:-1]


def along_x(field):
    return 0.5 * (east_of(field) - west_of(field))


def along_y(field):
    return 0.5 * (north_of(field) - south_of(field))


def laplace(field):
    return east_of(field) + west_of(field) + north_of(field) + south_of(field) - 4.0 * centre(field)


def advance(padded, pushes, coriolis):
    height = padded[..., 0, :, :]
    zonal = padded[..., 1, :, :]
    merid = padded[..., 2, :, :]
    height_c = centre(height)
    zonal_c = centre(zonal)
    merid_c = centre(merid)
    flux_x = (DEPTH_MEAN + height) * zonal
    flux_y = (DEPTH_MEAN + height) * merid
    height_new = (
        height_c
        - COURANT * (along_x(flux_x) + along_y(flux_y))
        + DIFFUSION * laplace(height)
        + FORCE_STEP * pushes
    )
    zonal_new = (
        zonal_c
        - COURANT
        * (GRAVITY * along_x(height) + zonal_c * along_x(zonal) + merid_c * along_y(zonal))
        + COURANT * coriolis * merid_c
        + DIFFUSION * laplace(zonal)
    )
    merid_new = (
        merid_c
        - COURANT
        * (GRAVITY * along_y(height) + zonal_c * along_x(merid) + merid_c * along_y(merid))
        - COURANT * coriolis * zonal_c
        + DIFFUSION * laplace(merid)
    )
    return jnp.stack([height_new, zonal_new, merid_new], axis=-3)


def coriolis_rows(start, count, total):
    rows = start + jnp.arange(count, dtype=jnp.float32)
    return (CORIOLIS_MAX * (2.0 * (rows + 0.5) / total - 1.0))[:, None]


def ensemble_weights(gram, innovation_sum, members):
    identity = jnp.eye(members, dtype=jnp.float32)
    amat = (members - 1) * identity + gram
    scale = jnp.sqrt(jnp.sum(amat * amat))
    upper = amat / scale
    lower = identity
    for repeat in range(NS_ITERS):
        factor = 1.5 * identity - 0.5 * jnp.dot(lower, upper, precision=PRECISE)
        upper = jnp.dot(upper, factor, precision=PRECISE)
        lower = jnp.dot(factor, lower, precision=PRECISE)
    root = lower / jnp.sqrt(scale)
    inverse = jnp.dot(root, root, precision=PRECISE)
    mean_shift = jnp.dot(inverse, innovation_sum, precision=PRECISE)
    return math.sqrt(members - 1) * root + mean_shift[:, None]


def shards(ocean_status, height_driver, obs_index, obs_value, obs_error):
    members = ocean_status.shape[0]
    lat_cells = ocean_status.shape[2]
    lon_cells = ocean_status.shape[3]
    total_rows = lat_cells * lax.axis_size("lat")
    first_row = lax.axis_index("lat") * lat_cells
    pushes = height_driver.astype(jnp.float32)
    coriolis = coriolis_rows(first_row.astype(jnp.float32), lat_cells, total_rows)
    fields = ocean_status
    for repeat in range(2):
        row_ext = with_halo(fields, (("lat", 2),), 1, False)
        padded = with_halo(row_ext, (("lon", 3),), 1, True)
        fields = advance(padded, pushes, coriolis)
    flat_height = fields[:, 0].reshape(members, lat_cells * lon_cells)
    measurement_readings = jnp.take(flat_height, obs_index.reshape(-1), axis=1)
    obs_mean = jnp.mean(measurement_readings, axis=0)
    obs_spread = measurement_readings - obs_mean
    innovation = obs_value.reshape(-1) - obs_mean
    inv_error = 1.0 / obs_error.reshape(-1)
    gram_part = jnp.dot(obs_spread * inv_error, obs_spread.T, precision=PRECISE)
    shift_part = jnp.dot(obs_spread, inv_error * innovation, precision=PRECISE)
    gram, innovation_sum = lax.psum((gram_part, shift_part), ("lon", "lat"))
    blending_coefficients = ensemble_weights(gram, innovation_sum, members)
    ens_mean = jnp.mean(fields, axis=0, keepdims=True)
    spread = fields - ens_mean
    return ens_mean + jnp.einsum("kfyx,km->mfyx", spread, blending_coefficients, precision=PRECISE)


def solution(mesh):
    return jax.shard_map(
        shards,
        mesh=mesh,
        in_specs=(
            P(None, None, "lat", "lon"),
            P(None, "lat", "lon"),
            P("lat", "lon", None),
            P("lat", "lon", None),
            P("lat", "lon", None),
        ),
        out_specs=P(None, None, "lat", "lon"),
        check_vma=False,
    )
```

profile of v0, /device:TPU:1, one launch (start us, length us, event | category | flops | bytes accessed | tf_op | source)
XLA Modules:
  0.0 348.9 jit_solution(597052594125909921)
XLA Ops:
  6.5 6.2 %fusion.69 = (f32[128,3,1,512]{3,2,1,0:T(1,128)S(1)}, f32[128,3,1,512]{3,2,1,0:T(1,128)S(1)}) fusion(f32[128,3,8,512]{3,2,1,0:T(8,128)} %param.5), kind=kLoop, calls=%fused_computation.129 | loop fusion | bytes 3145728 | tf_op jit(solution)/shard_map/slice | solution.py:24
  12.8 4.0 %collective-permute-start = (f32[128,3,1,512]{3,0,2,1:T(8,128)S(1)}, f32[128,3,1,512]{3,0,2,1:T(8,128)S(1)}, u32[]{:S(2)}, u32[]{:S(2)}) collective-permute-start(f32[128,3,1,512]{3,0,2,1:T(8,128)S(1)} %copy.39), channel_id=1, source_target_pairs={{0,1},{1,2},{2,3},{3,4},{4,5},{5,6},{6,7},{8,9},{9,10},{10,11},{11... | collective-permute-start | bytes 2359304 | tf_op jit(solution)/shard_map/ppermute | solution.py:28
  16.9 1.3 collective-permute-start.1
  18.2 31.6 %collective-permute-done = f32[128,3,1,512]{3,0,2,1:T(8,128)S(1)} collective-permute-done((f32[128,3,1,512]{3,0,2,1:T(8,128)S(1)}, f32[128,3,1,512]{3,0,2,1:T(8,128)S(1)}, u32[]{:S(2)}, u32[]{:S(2)}) %collective-permute-start) | collective-permute-done | bytes 786464 | tf_op jit(solution)/shard_map/ppermute | solution.py:28
  49.9 6.4 %constant_dynamic-update-slice_fusion.1 = f32[128,3,10,512]{3,0,2,1:T(8,128)S(1)} fusion(f32[128,3,10,512]{3,0,2,1:T(8,128)S(1)} %constant_dynamic-update-slice_fusion.2, f32[128,3,8,512]{3,2,1,0:T(8,128)} %param.5), kind=kLoop, calls=%fused_computation.106 | loop fusion | bytes 12582912
  56.4 2.5 fusion.68
  58.9 1.1 copy-done.4
  60.0 2.1 copy.23
  62.1 1.6 collective-permute-start.3
  63.7 0.6 copy.22
  64.3 1.3 collective-permute-start.2
  65.6 0.6 collective-permute-done.3
  66.2 1.9 copy.25
  68.1 1.9 copy.24
  70.1 7.5 %pad_maximum_fusion = f32[128,3,10,514]{3,0,2,1:T(8,128)S(1)} fusion(f32[128,3,10,1]{3,0,2,1:T(8,128)} %copy.25, f32[128,3,10,512]{3,0,2,1:T(8,128)} %copy-done.4, f32[128,3,10,1]{3,0,2,1:T(8,128)} %copy.24), kind=kLoop, calls=%fused_computation.1 | loop fusion | flops 3947520 | bytes 15790080 | tf_op jit(solution)/shard_map/concatenate | solution.py:26
  77.5 2.4 slice_bitcast_fusion.5
  79.9 3.3 add_multiply_fusion.3
  83.2 10.2 %add_bitcast_fusion.3 = (f32[128,1,8,512]{3,0,2,1:T(8,128)S(1)}, f32[128,1,8,512]{3,0,2,1:T(8,128)S(1)}) fusion(f32[128,10,514]{2,0,1:T(8,128)} %get-tuple-element.18, f32[128,10,514]{2,0,1:T(8,128)S(1)} %get-tuple-element.17, f32[128,10,514]{2,0,1:T(8,128)S(1)} %get-tuple-element.16, f32[8]{0:T(128)S(1)} %add_multiply_fusion.4), kind=kLoop, calls=%fused_computation.37 | loop fusion | flops 22020096 | bytes 33554464 | tf_op jit(solution)/shard_map/stack | solution.py:98
  93.4 6.6 %fusion.17 = f32[128,1,8,512]{3,0,2,1:T(8,128)S(1)} fusion(f32[128,10,514]{2,0,1:T(8,128)} %get-tuple-element.15, f32[128,10,514]{2,0,1:T(8,128)S(1)} %copy-done.7, f32[128,10,514]{2,0,1:T(8,128)S(1)} %get-tuple-element.16, bf16[128,8,512]{2,1,0:T(8,128)(2,1)S(1)} %copy-done.8), kind=kLoop, calls=%fused_computation.32 | loop fusion | flops 7864320 | bytes 22020096 | tf_op jit(solution)/shard_map/stack | solution.py:98
  100.3 1.3 collective-permute-start.5
  101.6 4.8 %collective-permute-start.4 = (f32[128,3,1,512]{3,0,2,1:T(8,128)S(1)}, f32[128,3,1,512]{3,0,2,1:T(8,128)S(1)}, u32[]{:S(2)}, u32[]{:S(2)}) collective-permute-start(f32[128,3,1,512]{3,0,2,1:T(8,128)S(1)} %get-tuple-element.23), channel_id=1, source_target_pairs={{0,1},{1,2},{2,3},{3,4},{4,5},{5,6},{6,7},{8,9},{9,10},{10,11},{11... | collective-permute-start | bytes 2359304 | tf_op jit(solution)/shard_map/ppermute | solution.py:28
  106.4 15.6 %collective-permute-done.5 = f32[128,3,1,512]{3,0,2,1:T(8,128)S(1)} collective-permute-done((f32[128,3,1,512]{3,0,2,1:T(8,128)S(1)}, f32[128,3,1,512]{3,0,2,1:T(8,128)S(1)}, u32[]{:S(2)}, u32[]{:S(2)}) %collective-permute-start.5) | collective-permute-done | bytes 786464 | tf_op jit(solution)/shard_map/ppermute | solution.py:30
  122.0 17.5 %collective-permute-done.4 = f32[128,3,1,512]{3,0,2,1:T(8,128)S(1)} collective-permute-done((f32[128,3,1,512]{3,0,2,1:T(8,128)S(1)}, f32[128,3,1,512]{3,0,2,1:T(8,128)S(1)}, u32[]{:S(2)}, u32[]{:S(2)}) %collective-permute-start.4) | collective-permute-done | bytes 786464 | tf_op jit(solution)/shard_map/ppermute | solution.py:28
  139.5 2.7 pad_maximum_fusion.8
  142.2 2.1 copy.28
  144.3 0.6 collective-permute-start.7
  144.9 2.1 copy.27
  147.0 1.4 collective-permute-start.6
  148.4 1.9 copy.30
  150.3 1.9 copy.29
  152.2 8.8 %pad_maximum_fusion.1 = f32[128,3,10,514]{3,0,2,1:T(8,128)S(1)} fusion(f32[128,3,10,1]{3,0,2,1:T(8,128)} %copy.30, f32[128,3,1,512]{3,0,2,1:T(8,128)S(1)} %collective-permute-done.5, f32[128,1,8,512]{3,0,2,1:T(8,128)} %copy-done.2, f32[128,1,8,512]{3,0,2,1:T(8,128)S(1)} %get-tuple-element.7, f32[128,1,8,512]{3,0,2,1:T(8,128)} %copy-done.3, ...), kind=kLoop, calls=%fused_computation.2 | loop fusion | flops 11842560 | bytes 15790080 | tf_op jit(solution)/shard_map/concatenate | solution.py:26
  161.0 3.6 %slice_bitcast_fusion.2 = (f32[128,10,514]{2,0,1:T(8,128)S(1)}, f32[128,10,514]{2,0,1:T(8,128)}, f32[128,10,514]{2,0,1:T(8,128)}) fusion(f32[128,3,10,514]{3,0,2,1:T(8,128)S(1)} %pad_maximum_fusion.1), kind=kLoop, calls=%fused_computation.10 | loop fusion | bytes 15790080 | tf_op jit(solution)/shard_map/squeeze | solution.py:70
  164.7 0.6 add_multiply_fusion.1
  165.3 0.6 copy-done.9
  165.9 5.2 %fusion.11 = f32[128,8,512]{2,0,1:T(8,128)} fusion(f32[128,10,514]{2,0,1:T(8,128)S(1)} %get-tuple-element.10, f32[128,10,514]{2,0,1:T(8,128)S(1)} %get-tuple-element.9, f32[128,10,514]{2,0,1:T(8,128)S(1)} %get-tuple-element.11, bf16[128,8,512]{2,1,0:T(8,128)(2,1)S(1)} %copy-done.9), kind=kLoop, calls=%fused_computation.24 | loop fusion | flops 7864320 | bytes 22020096 | tf_op jit(solution)/shard_map/add | solution.py:79
  171.1 2.9 copy.31
  174.0 14.3 %add_bitcast_fusion.1 = (f32[128,1,8,512]{3,0,2,1:T(8,128)S(1)}, f32[128,1,8,512]{3,0,2,1:T(8,128)S(1)}) fusion(f32[128,10,514]{2,0,1:T(8,128)} %get-tuple-element.13, f32[128,10,514]{2,0,1:T(8,128)} %get-tuple-element.12, f32[128,10,514]{2,0,1:T(8,128)S(1)} %get-tuple-element.11, f32[8]{0:T(128)S(1)} %add_multiply_fusion.4), kind=kLoop, calls=%fused_computation.35 | loop fusion | flops 22020096 | bytes 33554464 | tf_op jit(solution)/shard_map/stack | solution.py:98
  188.3 0.9 fusion.2
  189.7 0.6 copy-done.6
  190.3 2.2 gather_fusion
  192.6 1.0 fusion.38
  193.9 40.9 %psum.15 = f32[128]{0:T(128)S(1)} all-reduce(f32[128]{0:T(128)S(1)} %convolution_bitcast_fusion.1), channel_id=1, replica_groups=mesh['lon'=4,'lat'=8] {'lon','lat'}, use_global_device_ids=true, to_apply=%region_4.5 | all-reduce | flops 128 | bytes 1024 | tf_op jit(solution)/shard_map/psum | solution.py:143
  234.8 79.0 %all-reduce.2.cloned.1.call-done = f32[128,128]{1,0:T(8,128)} async-done(((f32[128,128]{1,0:T(8,128)}), f32[128,128]{1,0:T(8,128)}) %all-reduce.2.cloned.1.call-update) | async-done | bytes 65552 | tf_op jit(solution)/shard_map/psum | solution.py:143
  313.8 1.5 multiply_reduce_fusion
  316.1 1.0 fusion.31
  317.4 1.1 fusion.52
  326.9 8.5 %fusion.3 = f32[128,3,8,512]{3,0,2,1:T(8,128)S(1)} fusion(f32[128,1,8,512]{3,0,2,1:T(8,128)} %copy-done.6, f32[128,1,8,512]{3,0,2,1:T(8,128)} %copy-done.5, f32[128,1,8,512]{3,0,2,1:T(8,128)S(1)} %bitcast.158, f32[3,8,512]{2,1,0:T(8,128)S(1)} %broadcast_multiply_fusion, f32[128,128]{1,0:T(8,128)S(1)} %convolution_divide_fusion, ...), kind=kOutput, calls=%fused_computation.7 | convolution fusion | flops 2422243328 | bytes 12698112 | tf_op jit(solution)/shard_map/kfyx,km->mfyx/dot_general | solution.py:147
  335.4 6.5 %copy.33 = f32[128,3,8,512]{3,2,1,0:T(8,128)} copy(f32[128,3,8,512]{3,0,2,1:T(8,128)S(1)} %fusion.3) | data formatting | bytes 12582912 | tf_op jit(solution)/shard_map/add | solution.py:147
  (86 shorter events, 9.7 us)
Async XLA Ops:
  6.5 307.3 %all-reduce.2.cloned.1.call-start = ((), (), s32[]{:S(2)}) async-start(), calls=%async_computation | async-start | bytes 131072 | tf_op jit(solution)/shard_map/psum | solution.py:143
  12.8 37.0 %collective-permute-start = (f32[128,3,1,512]{3,0,2,1:T(8,128)S(1)}, f32[128,3,1,512]{3,0,2,1:T(8,128)S(1)}, u32[]{:S(2)}, u32[]{:S(2)}) collective-permute-start(f32[128,3,1,512]{3,0,2,1:T(8,128)S(1)} %copy.39), channel_id=1, source_target_pairs={{0,1},{1,2},{2,3},{3,4},{4,5},{5,6},{6,7},{8,9},{9,10},{10,11},{11... | collective-permute-start | bytes 2359304 | tf_op jit(solution)/shard_map/ppermute | solution.py:28
  16.9 39.4 %collective-permute-start.1 = (f32[128,3,1,512]{3,0,2,1:T(8,128)S(1)}, f32[128,3,1,512]{3,0,2,1:T(8,128)S(1)}, u32[]{:S(2)}, u32[]{:S(2)}) collective-permute-start(f32[128,3,1,512]{3,0,2,1:T(8,128)S(1)} %copy.40), channel_id=1, source_target_pairs={{1,0},{2,1},{3,2},{4,3},{5,4},{6,5},{7,6},{9,8},{10,9},{11,10},{12... | collective-permute-start | bytes 2359304 | tf_op jit(solution)/shard_map/ppermute | solution.py:30
  56.4 3.6 %copy-start.4 = (f32[128,3,10,512]{3,0,2,1:T(8,128)}, f32[128,3,10,512]{3,0,2,1:T(8,128)S(1)}, u32[]{:S(2)}) copy-start(f32[128,3,10,512]{3,0,2,1:T(8,128)S(1)} %constant_dynamic-update-slice_fusion) | copy-start | bytes 23592964
  62.1 4.1 %collective-permute-start.3 = (f32[128,3,10,1]{0,3,2,1:T(1,128)S(1)}, f32[128,3,10,1]{0,3,2,1:T(1,128)S(1)}, u32[]{:S(2)}, u32[]{:S(2)}) collective-permute-start(f32[128,3,10,1]{0,3,2,1:T(1,128)S(1)} %copy.23), channel_id=1, source_target_pairs={{8,0},{16,8},{24,16},{0,24},{9,1},{17,9},{25,17},{1,25},{10,2},{18... | collective-permute-start | bytes 46088 | tf_op jit(solution)/shard_map/ppermute | solution.py:30
  64.3 3.8 %collective-permute-start.2 = (f32[128,3,10,1]{0,3,2,1:T(1,128)S(1)}, f32[128,3,10,1]{0,3,2,1:T(1,128)S(1)}, u32[]{:S(2)}, u32[]{:S(2)}) collective-permute-start(f32[128,3,10,1]{0,3,2,1:T(1,128)S(1)} %copy.22), channel_id=1, source_target_pairs={{0,8},{8,16},{16,24},{24,0},{1,9},{9,17},{17,25},{25,1},{2,10},{10... | collective-permute-start | bytes 46088 | tf_op jit(solution)/shard_map/ppermute | solution.py:28
  83.2 10.2 %copy-start.7 = (f32[128,10,514]{2,0,1:T(8,128)S(1)}, f32[128,10,514]{2,0,1:T(8,128)}, u32[]{:S(2)}) copy-start(f32[128,10,514]{2,0,1:T(8,128)} %get-tuple-element.14) | copy-start | bytes 7895044
  83.2 10.2 %copy-start.8 = (bf16[128,8,512]{2,1,0:T(8,128)(2,1)S(1)}, bf16[128,8,512]{2,1,0:T(8,128)(2,1)}, u32[]{:S(2)}) copy-start(bf16[128,8,512]{2,1,0:T(8,128)(2,1)} %param.6) | copy-start | bytes 3145732
  93.4 46.1 %copy-start.2 = (f32[128,1,8,512]{3,0,2,1:T(8,128)}, f32[128,1,8,512]{3,0,2,1:T(8,128)S(1)}, u32[]{:S(2)}) copy-start(f32[128,1,8,512]{3,0,2,1:T(8,128)S(1)} %get-tuple-element.8) | copy-start | bytes 6291460
  100.1 39.4 %copy-start.3 = (f32[128,1,8,512]{3,0,2,1:T(8,128)}, f32[128,1,8,512]{3,0,2,1:T(8,128)S(1)}, u32[]{:S(2)}) copy-start(f32[128,1,8,512]{3,0,2,1:T(8,128)S(1)} %fusion.17) | copy-start | bytes 6291460
  100.1 6.3 %copy-start.11 = (s32[1,1,64]{2,1,0:T(1,128)S(1)}, s32[1,1,64]{2,1,0:T(1,128)}, u32[]{:S(2)}) copy-start(s32[1,1,64]{2,1,0:T(1,128)} %param.7) | copy-start | bytes 772
  100.1 6.3 %copy-start.12 = (f32[1,1,64]{2,1,0:T(1,128)S(1)}, f32[1,1,64]{2,1,0:T(1,128)}, u32[]{:S(2)}) copy-start(f32[1,1,64]{2,1,0:T(1,128)} %param.9) | copy-start | bytes 772
  100.3 21.7 %collective-permute-start.5 = (f32[128,3,1,512]{3,0,2,1:T(8,128)S(1)}, f32[128,3,1,512]{3,0,2,1:T(8,128)S(1)}, u32[]{:S(2)}, u32[]{:S(2)}) collective-permute-start(f32[128,3,1,512]{3,0,2,1:T(8,128)S(1)} %get-tuple-element.24), channel_id=1, source_target_pairs={{1,0},{2,1},{3,2},{4,3},{5,4},{6,5},{7,6},{9,8},{10,9},{11,10},{12... | collective-permute-start | bytes 2359304 | tf_op jit(solution)/shard_map/ppermute | solution.py:30
  101.6 37.9 %collective-permute-start.4 = (f32[128,3,1,512]{3,0,2,1:T(8,128)S(1)}, f32[128,3,1,512]{3,0,2,1:T(8,128)S(1)}, u32[]{:S(2)}, u32[]{:S(2)}) collective-permute-start(f32[128,3,1,512]{3,0,2,1:T(8,128)S(1)} %get-tuple-element.23), channel_id=1, source_target_pairs={{0,1},{1,2},{2,3},{3,4},{4,5},{5,6},{6,7},{8,9},{9,10},{10,11},{11... | collective-permute-start | bytes 2359304 | tf_op jit(solution)/shard_map/ppermute | solution.py:28
  139.5 2.7 copy-start.10
  144.3 4.1 %collective-permute-start.7 = (f32[128,3,10,1]{0,3,2,1:T(1,128)S(1)}, f32[128,3,10,1]{0,3,2,1:T(1,128)S(1)}, u32[]{:S(2)}, u32[]{:S(2)}) collective-permute-start(f32[128,3,10,1]{0,3,2,1:T(1,128)S(1)} %copy.28), channel_id=1, source_target_pairs={{8,0},{16,8},{24,16},{0,24},{9,1},{17,9},{25,17},{1,25},{10,2},{18... | collective-permute-start | bytes 46088 | tf_op jit(solution)/shard_map/ppermute | solution.py:30
  147.0 3.3 collective-permute-start.6
  164.7 1.2 copy-start.9
  174.0 14.3 %copy-start = (f32[128,8,512]{2,0,1:T(8,128)S(1)}, f32[128,8,512]{2,0,1:T(8,128)}, u32[]{:S(2)}) copy-start(f32[128,8,512]{2,0,1:T(8,128)} %fusion.11) | copy-start | bytes 6291460
  188.3 1.4 copy-start.5
  188.3 2.0 copy-start.6
  188.3 5.4 %copy-start.13 = (f32[1,1,64]{2,1,0:T(1,128)S(1)}, f32[1,1,64]{2,1,0:T(1,128)}, u32[]{:S(2)}) copy-start(f32[1,1,64]{2,1,0:T(1,128)} %param.8) | copy-start | bytes 772
  322.2 4.7 %copy-start.1 = (f32[128,8,512]{2,0,1:T(8,128)S(1)}, f32[128,8,512]{2,0,1:T(8,128)}, u32[]{:S(2)}) copy-start(f32[128,8,512]{2,0,1:T(8,128)} %fusion.11) | copy-start | bytes 6291460
Sparse Core Ops, SparseCore 0:
  193.8 120.0 all-reduce.1
where the time goes:
time: 355 us; the launch traced here: 349 us
  waiting for transfers between devices  144 us (41%)
  other arithmetic  61.9 us (17%)
  local copies, waits for them, and re-layouts  50.4 us (14%)
  blocking collectives  40.9 us (12%)
  matrix products  20.1 us (6%)
  starting transfers between devices  16.3 us (5%)
  between operations  15 us (4%)
    psum x1, waiting for transfers between devices, shards(): gram, innovation_sum = lax.psum((gram_part, shift_part), ('lon', 'lat'))  79 us
    ppermute x4, waiting for transfers between devices, with_halo(): lax.ppermute(tail, axis, [(i, (i + 1) % count) for i in range(ends)])  49.1 us
    psum x1, blocking collectives, shards(): gram, innovation_sum = lax.psum((gram_part, shift_part), ('lon', 'lat'))  40.9 us
    another operation x3, other arithmetic, advance(): return jnp.stack([height_new, zonal_new, merid_new], axis=-3)  31 us
    concatenate x2, other arithmetic, with_halo(): jnp.concatenate([lax.ppermute(tail, axis, [(i, (i + 1) % count) for i in...  16.3 us
    ppermute x4, waiting for transfers between devices, with_halo(): lax.ppermute(head, axis, [((i + 1) % count, i) for i in range(ends)])  16.2 us
    ppermute x4, starting transfers between devices, with_halo(): lax.ppermute(tail, axis, [(i, (i + 1) % count) for i in range(ends)])  11.5 us
    slice x3, local copies, waits for them, and re-layouts, with_halo(): head = lax.slice_in_dim(cells, 0, width, axis=dim)  10.4 us
  transfers between devices with their start and end apart: 9, of which 5 were waited for; matrix products, arithmetic and copies ran while one was open for 4% of the time, Pallas kernels for 0%

commit v1 on v0

v1 whole, which is shorter than its diff:
```python
import functools
import math

import jax
import jax.numpy as jnp
from jax import lax
from jax.experimental import pallas as pl
from jax.experimental.pallas import tpu as pltpu
from jax.sharding import PartitionSpec as P

NS_ITERS = 14
COURANT = 0.2
DIFFUSION = 0.1
FORCE_STEP = 0.5
CORIOLIS_MAX = 0.3
CHUNK = 16
LANES = 128
MESH = pl.DeviceIdType.MESH


def doublings(count):
    return [1 << b for b in range(count.bit_length() - 1)]


def parts_of(x, count):
    parts = []
    for _ in range(count):
        parts.append(x.astype(jnp.bfloat16))
        x = x - parts[-1].astype(jnp.float32)
    return parts


def product(a, b):
    rows, columns = a.shape[0], b.shape[1]
    whole = jnp.dot(jnp.concatenate(parts_of(a, 2), axis=0), jnp.concatenate(parts_of(b, 2), axis=1),
                    preferred_element_type=jnp.float32)
    return (whole[:rows, :columns] + whole[:rows, columns:]) + (whole[rows:, :columns] + whole[rows:, columns:])


def forecast_kernel(n_lat, n_lon, state_hbm, force_ref, index_ref, value_ref, error_ref, fore_hbm, sums_ref,
                    raw, ext, cols_out, cols_in, fore, onehot, readings, acc, acc_in,
                    in_sem, out_sem, row_send, row_recv, col_send, col_recv, sum_send, sum_recv):
    chunks = raw.shape[0]
    members = chunks * CHUNK
    rows, width = raw.shape[3], raw.shape[4]
    lat, lon = lax.axis_index("lat"), lax.axis_index("lon")
    east = (lat, lax.rem(lon + 1, n_lon))
    west = (lat, lax.rem(lon + n_lon - 1, n_lon))
    has_south, has_north = lat > 0, lat < n_lat - 1
    south, north = (jnp.maximum(lat - 1, 0), lon), (jnp.minimum(lat + 1, n_lat - 1), lon)

    def dev(place):
        return {"lat": place[0], "lon": place[1]}

    partners = [(lat, lon ^ d) for d in doublings(n_lon)] + [(lat ^ d, lon) for d in doublings(n_lat)]
    far = [(lat, lon ^ d) for d in doublings(n_lon)[1:]] + [(lat ^ d, lon) for d in doublings(n_lat)[1:]]

    def load(c):
        return pltpu.make_async_copy(state_hbm.at[pl.ds(c * CHUNK, CHUNK)], raw.at[c], in_sem.at[c])

    @pl.loop(0, chunks)
    def _(c):
        load(c).start()

    barrier = pltpu.get_barrier_semaphore()
    for place in [east, west] + far:
        pl.semaphore_signal(barrier, inc=1, device_id=dev(place), device_id_type=MESH)

    @pl.when(has_south)
    def _():
        pl.semaphore_signal(barrier, inc=1, device_id=dev(south), device_id_type=MESH)

    @pl.when(has_north)
    def _():
        pl.semaphore_signal(barrier, inc=1, device_id=dev(north), device_id_type=MESH)

    pl.semaphore_wait(barrier, 2 + len(far) + has_south.astype(jnp.int32) + has_north.astype(jnp.int32))

    def row_copy(step, c, side):
        return pltpu.make_async_remote_copy(
            src_ref=ext.at[step, c, :, rows if side == 0 else 1],
            dst_ref=ext.at[step, c, :, 0 if side == 0 else rows + 1],
            send_sem=row_send.at[step, side, c], recv_sem=row_recv.at[step, side, c],
            device_id=dev(north if side == 0 else south), device_id_type=MESH)

    def col_copy(step, c, side):
        return pltpu.make_async_remote_copy(
            src_ref=cols_out.at[step, side, c], dst_ref=cols_in.at[step, side, c],
            send_sem=col_send.at[step, side, c], recv_sem=col_recv.at[step, side, c],
            device_id=dev(east if side == 0 else west), device_id_type=MESH)

    lane = lax.broadcasted_iota(jnp.int32, (CHUNK, LANES), 1)
    wide = lax.broadcasted_iota(jnp.int32, (CHUNK, width), 1)

    def send(step, c):
        @pl.when(has_north)
        def _():
            row_copy(step, c, 0).start()

        @pl.when(has_south)
        def _():
            row_copy(step, c, 1).start()

        last = jnp.zeros((CHUNK, LANES), jnp.float32)
        first = last
        for f in range(3):
            for r in range(rows):
                j = f * rows + r
                last = jnp.where(lane == j, ext[step, c, f, r + 1, :, width - 1:width], last)
                first = jnp.where(lane == j, ext[step, c, f, r + 1, :, 0:1], first)
        cols_out[step, 0, c] = last
        cols_out[step, 1, c] = first
        col_copy(step, c, 0).start()
        col_copy(step, c, 1).start()

    def receive(step, c):
        @pl.when(has_south)
        def _():
            row_copy(step, c, 0).wait_recv()

        @pl.when(has_north)
        def _():
            row_copy(step, c, 1).wait_recv()

        col_copy(step, c, 0).wait_recv()
        col_copy(step, c, 1).wait_recv()

    @pl.when(lat == 0)
    def _():
        for step in range(2):
            @pl.loop(0, chunks)
            def _(c):
                ext[step, c, :, 0] = jnp.zeros((3, CHUNK, width), jnp.float32)

    @pl.when(lat == n_lat - 1)
    def _():
        for step in range(2):
            @pl.loop(0, chunks)
            def _(c):
                ext[step, c, :, rows + 1] = jnp.zeros((3, CHUNK, width), jnp.float32)

    @pl.loop(0, chunks)
    def _(c):
        load(c).wait()
        for f in range(3):
            ext[0, c, f, pl.ds(1, rows)] = jnp.swapaxes(raw[c, :, f], 0, 1)
        send(0, c)

    total_rows = float(n_lat * rows)
    first_row = (lat * rows).astype(jnp.float32)

    def advance(step, c, put):
        pushes = jnp.swapaxes(force_ref[pl.ds(c * CHUNK, CHUNK)].astype(jnp.float32), 0, 1)
        from_west = cols_in[step, 0, c]
        from_east = cols_in[step, 1, c]
        for r in range(rows):
            coriolis = CORIOLIS_MAX * (2.0 * (first_row + (r + 0.5)) / total_rows - 1.0)

            def around(f):
                mid = ext[step, c, f, r + 1]
                j = f * rows + r
                e = jnp.where(wide == width - 1, from_east[:, j:j + 1], pltpu.roll(mid, width - 1, 1))
                w = jnp.where(wide == 0, from_west[:, j:j + 1], pltpu.roll(mid, 1, 1))
                return mid, e, w, ext[step, c, f, r + 2], ext[step, c, f, r]

            h, he, hw, hn, hs = around(0)
            u, ue, uw, un, us = around(1)
            v, ve, vw, vn, vs = around(2)
            half = 0.5 * COURANT
            h_new = (h - half * (((1.0 + he) * ue - (1.0 + hw) * uw) + ((1.0 + hn) * vn - (1.0 + hs) * vs))
                     + DIFFUSION * (he + hw + hn + hs - 4.0 * h) + FORCE_STEP * pushes[r])
            u_new = (u - half * ((he - hw) + u * (ue - uw) + v * (un - us))
                     + COURANT * coriolis * v + DIFFUSION * (ue + uw + un + us - 4.0 * u))
            v_new = (v - half * ((hn - hs) + u * (ve - vw) + v * (vn - vs))
                     - COURANT * coriolis * u + DIFFUSION * (ve + vw + vn + vs - 4.0 * v))
            put(r, h_new, u_new, v_new)

    @pl.loop(0, chunks)
    def _(c):
        receive(0, c)

        def put(r, *new):
            for f in range(3):
                ext[1, c, f, r + 1] = new[f]

        advance(0, c, put)
        send(1, c)

    for r in range(rows):
        cell = lax.broadcasted_iota(jnp.int32, (width, LANES), 0) + r * width
        onehot[r] = jnp.where(cell == index_ref[0:1, :], 1.0, 0.0).astype(jnp.bfloat16)

    def save(c):
        return pltpu.make_async_copy(fore.at[c], fore_hbm.at[c], out_sem.at[c])

    @pl.loop(0, chunks)
    def _(c):
        receive(1, c)

        def put(r, *new):
            for f in range(3):
                fore[c, f, r] = new[f]

        advance(1, c, put)
        save(c).start()
        seen = jnp.zeros((CHUNK, LANES), jnp.float32)
        for r in range(rows):
            picked = jnp.dot(jnp.concatenate(parts_of(fore[c, 0, r], 3), axis=0), onehot[r],
                             preferred_element_type=jnp.float32)
            seen += (picked[:CHUNK] + picked[CHUNK:2 * CHUNK]) + picked[2 * CHUNK:]
        readings[c] = seen

    seen = readings[...].reshape(members, LANES)
    mean = jnp.mean(seen, axis=0, keepdims=True)
    spread = seen - mean
    inv = 1.0 / error_ref[0:1, :]
    innovation = inv * (value_ref[0:1, :] - mean)
    left = jnp.concatenate([spread * inv, jnp.broadcast_to(innovation, (8, LANES))], axis=0)
    acc[0] = product(left, spread.T)
    swaps = [pltpu.make_async_remote_copy(
        src_ref=acc.at[s], dst_ref=acc_in.at[s], send_sem=sum_send.at[s], recv_sem=sum_recv.at[s],
        device_id=dev(place), device_id_type=MESH) for s, place in enumerate(partners)]
    for s, swap in enumerate(swaps):
        swap.start()
        swap.wait_recv()
        acc[s + 1] = acc[s] + acc_in[s]
    sums_ref[...] = acc[len(swaps)]
    for swap in swaps:
        swap.wait_send()

    @pl.loop(0, chunks)
    def _(c):
        save(c).wait()
        for step in range(2):
            @pl.when(has_north)
            def _():
                row_copy(step, c, 0).wait_send()

            @pl.when(has_south)
            def _():
                row_copy(step, c, 1).wait_send()

            col_copy(step, c, 0).wait_send()
            col_copy(step, c, 1).wait_send()


def analysis_kernel(sums_ref, fore_ref, out_ref, mix):
    members = sums_ref.shape[1]
    rows = fore_ref.shape[2]
    width = fore_ref.shape[4]

    @pl.when(pl.program_id(0) == 0)
    def _():
        eye = (lax.broadcasted_iota(jnp.int32, (members, members), 0)
               == lax.broadcasted_iota(jnp.int32, (members, members), 1)).astype(jnp.float32)
        amat = (members - 1) * eye + sums_ref[:members]
        scale = jnp.sqrt(jnp.sum(jnp.sum(amat * amat, axis=1, keepdims=True), axis=0, keepdims=True))

        def turn(_, pair):
            upper, lower = pair
            factor = 1.5 * eye - 0.5 * product(lower, upper)
            return product(upper, factor), product(factor, lower)

        _, lower = lax.fori_loop(0, NS_ITERS, turn, (amat / scale, eye))
        root = lower / jnp.sqrt(scale)
        inverse = product(root, root)
        shift = product(sums_ref[members:], inverse.T)
        weights = math.sqrt(members - 1) * root.T + shift[0:1, :]
        high = weights.astype(jnp.bfloat16)
        low = (weights - high.astype(jnp.float32)).astype(jnp.bfloat16)
        mix[:members, :members] = high
        mix[:members, members:] = high
        mix[members:, :members] = low
        mix[members:, members:] = jnp.zeros_like(low)

    for r in range(rows):
        cells = fore_ref[:, 0, r].reshape(members, width)
        mean = jnp.mean(cells, axis=0, keepdims=True)
        spread = cells - mean
        high = spread.astype(jnp.bfloat16)
        low = (spread - high.astype(jnp.float32)).astype(jnp.bfloat16)
        both = jnp.dot(mix[...], jnp.concatenate([high, low], axis=0), preferred_element_type=jnp.float32)
        out_ref[:, 0, r, :] = mean + both[:members] + both[members:]


def shards(n_lat, n_lon, ocean_status, height_driver, obs_index, obs_value, obs_error):
    members, fields, rows, width = ocean_status.shape
    chunks = members // CHUNK
    spare = LANES - obs_index.shape[-1]

    def flat(array, fill):
        return jnp.pad(array.reshape(1, -1), ((0, 0), (0, spare)), constant_values=fill)

    vmem = pl.BlockSpec(memory_space=pltpu.VMEM)
    anywhere = pl.BlockSpec(memory_space=pl.ANY)
    stages = len(doublings(n_lon)) + len(doublings(n_lat))
    dma = pltpu.SemaphoreType.DMA
    f32 = jnp.float32
    block = (chunks, fields, rows, CHUNK, width)
    fore, sums = pl.pallas_call(
        functools.partial(forecast_kernel, n_lat, n_lon),
        out_shape=(jax.ShapeDtypeStruct(block, f32), jax.ShapeDtypeStruct((members + 8, members), f32)),
        in_specs=[anywhere, vmem, vmem, vmem, vmem],
        out_specs=(anywhere, vmem),
        scratch_shapes=[
            pltpu.VMEM((chunks, CHUNK, fields, rows, width), f32),
            pltpu.VMEM((2, chunks, fields, rows + 2, CHUNK, width), f32),
            pltpu.VMEM((2, 2, chunks, CHUNK, LANES), f32),
            pltpu.VMEM((2, 2, chunks, CHUNK, LANES), f32),
            pltpu.VMEM(block, f32),
            pltpu.VMEM((rows, width, LANES), jnp.bfloat16),
            pltpu.VMEM((chunks, CHUNK, LANES), f32),
            pltpu.VMEM((stages + 1, members + 8, members), f32),
            pltpu.VMEM((stages, members + 8, members), f32),
            dma((chunks,)), dma((chunks,)),
            dma((2, 2, chunks)), dma((2, 2, chunks)),
            dma((2, 2, chunks)), dma((2, 2, chunks)),
            dma((stages,)), dma((stages,)),
        ],
        compiler_params=pltpu.CompilerParams(collective_id=0, has_side_effects=True, vmem_limit_bytes=52 << 20),
        name="forecast",
    )(ocean_status, height_driver, flat(obs_index, -1), flat(obs_value, 0), flat(obs_error, 1))
    return pl.pallas_call(
        analysis_kernel,
        grid=(fields,),
        out_shape=jax.ShapeDtypeStruct(ocean_status.shape, f32),
        in_specs=[pl.BlockSpec((members + 8, members), lambda i: (0, 0)),
                  pl.BlockSpec((chunks, 1, rows, CHUNK, width), lambda i: (0, i, 0, 0, 0))],
        out_specs=pl.BlockSpec((members, 1, rows, width), lambda i: (0, i, 0, 0)),
        scratch_shapes=[pltpu.VMEM((2 * members, 2 * members), jnp.bfloat16)],
        compiler_params=pltpu.CompilerParams(vmem_limit_bytes=48 << 20),
        name="analysis",
    )(sums, fore)


def solution(mesh):
    return jax.shard_map(
        functools.partial(shards, mesh.shape["lat"], mesh.shape["lon"]),
        mesh=mesh,
        in_specs=(
            P(None, None, "lat", "lon"),
            P(None, "lat", "lon"),
            P("lat", "lon", None),
            P("lat", "lon", None),
            P("lat", "lon", None),
        ),
        out_specs=P(None, None, "lat", "lon"),
        check_vma=False,
    )
```

time: 355 us -> 109 us (0.31)
  the two profiles are of different devices: /device:TPU:1 before, /device:TPU:0 now
where the time goes in v1:
time: 109 us; the launch traced here: 108 us
  Pallas kernels  105 us (96%)
  local copies, waits for them, and re-layouts  3.2 us (3%)
    pallas_call x1, Pallas kernels, shards(): pl.pallas_call(functools.partial(forecast_kernel, n_lat, n_lon), out_shap...  90.9 us
    pallas_call x1, Pallas kernels, shards(): pl.pallas_call(analysis_kernel, grid=(fields,), out_shape=jax.ShapeDtypeS...  13.8 us

profile of v1, /device:TPU:0, one launch (start us, length us, event | category | flops | bytes accessed | tf_op | source)
XLA Modules:
  0.0 107.9 jit_solution(11148692459324756972)
XLA Ops:
  0.0 0.7 pad.11.index_ref
  0.7 0.7 pad.12.value_ref
  1.3 0.7 pad.13.error_ref
  2.0 0.0 copy-start
  2.0 1.2 %copy-done = bf16[128,8,512]{2,1,0:T(8,128)(2,1)S(1)} copy-done((bf16[128,8,512]{2,1,0:T(8,128)(2,1)S(1)}, bf16[128,8,512]{2,1,0:T(8,128)(2,1)}, u32[]{:S(2)}) %copy-start) | copy-done | bytes 1048600
  3.2 90.9 %forecast.1 = (f32[8,3,8,16,512]{4,3,2,1,0:T(8,128)}, f32[136,128]{1,0:T(8,128)S(1)}) custom-call(f32[128,3,8,512]{3,2,1,0:T(8,128)} %state_hbm.1, bf16[128,8,512]{2,1,0:T(8,128)(2,1)S(1)} %copy-done, s32[1,128]{1,0:T(1,128)S(1)} %pad.11.index_ref, f32[1,128]{1,0:T(1,128)S(1)} %pad.12.value_ref, f32[1,128]{1,0:T(1,128)S(1)} %pad.13.error_ref), custom_call_target="tpu_custom_call" | custom-call | tf_op jit(solution)/shard_map/forecast/pallas_call | solution.py:300
  94.1 13.8 %analysis.1 = f32[128,3,8,512]{3,2,1,0:T(8,128)} custom-call(f32[136,128]{1,0:T(8,128)S(1)} %get-tuple-element.7.sums_ref, f32[8,3,8,16,512]{4,3,2,1,0:T(8,128)} %get-tuple-element.8.fore_ref), custom_call_target="tpu_custom_call" | custom-call | tf_op jit(solution)/shard_map/analysis/pallas_call | solution.py:323
Async XLA Ops:
  2.0 1.2 %copy-start = (bf16[128,8,512]{2,1,0:T(8,128)(2,1)S(1)}, bf16[128,8,512]{2,1,0:T(8,128)(2,1)}, u32[]{:S(2)}) copy-start(bf16[128,8,512]{2,1,0:T(8,128)(2,1)} %force_ref.1) | copy-start | bytes 3145732

commit v2 on v1

--- a/solution.py
+++ b/solution.py
@@ -37,11 +37,46 @@
     return (whole[:rows, :columns] + whole[:rows, columns:]) + (whole[rows:, :columns] + whole[rows:, columns:])
 
 
-def forecast_kernel(n_lat, n_lon, state_hbm, force_ref, index_ref, value_ref, error_ref, fore_hbm, sums_ref,
-                    raw, ext, cols_out, cols_in, fore, onehot, readings, acc, acc_in,
-                    in_sem, out_sem, row_send, row_recv, col_send, col_recv, sum_send, sum_recv):
+def paired(a, b):
+    columns = b.shape[1]
+    terms = jnp.concatenate(parts_of(b, 2), axis=1)
+    whole = jnp.dot(jnp.concatenate(parts_of(a, 2), axis=1), jnp.concatenate([terms, terms], axis=0),
+                    preferred_element_type=jnp.float32)
+    return whole[:, :columns] + whole[:, columns:]
+
+
+def fold(sums):
+    members = sums.shape[1]
+    half = members // 2
+    row = lax.broadcasted_iota(jnp.int32, (half, members), 0)
+    column = lax.broadcasted_iota(jnp.int32, (half, members), 1)
+    corner = pltpu.roll(sums[half:members], half, 1)
+    mixed = jnp.where((column < half) & (row > column), corner, sums[:half])
+    diagonal = jnp.sum(jnp.where(row == column, corner, 0.0), axis=0, keepdims=True)
+    place = lax.broadcasted_iota(jnp.int32, (8, members), 0)
+    return jnp.concatenate([mixed, jnp.where(place == 0, sums[members:], diagonal)], axis=0)
+
+
+def unfold(folded):
+    half = folded.shape[0] - 8
+    members = 2 * half
+    row = lax.broadcasted_iota(jnp.int32, (members, members), 0)
+    column = lax.broadcasted_iota(jnp.int32, (members, members), 1)
+    upper = jnp.concatenate([folded[:half], jnp.zeros((half, members), jnp.float32)], axis=0)
+    lower = pltpu.roll(pltpu.roll(upper, half, 0), half, 1)
+    diagonal = pltpu.roll(folded[half:], half, 1)[1:2]
+    first = jnp.where((column >= half) | (row <= column), upper, upper.T)
+    last = jnp.where(column < half, upper.T,
+                     jnp.where(row > column, lower, jnp.where(row < column, lower.T, diagonal)))
+    return jnp.where(row < half, first, last)
+
+
+def forecast_kernel(n_lat, n_lon, state_hbm, force_hbm, index_ref, value_ref, error_ref, fore_hbm, sums_ref,
+                    raw, force, ext, cols_out, cols_in, fore, onehot, readings, acc, acc_in,
+                    in_sem, force_sem, out_sem, row_send, row_recv, col_send, col_recv, sum_send, sum_recv):
     chunks = raw.shape[0]
     members = chunks * CHUNK
+    sites = index_ref.shape[-1]
     rows, width = raw.shape[3], raw.shape[4]
     lat, lon = lax.axis_index("lat"), lax.axis_index("lon")
     east = (lat, lax.rem(lon + 1, n_lon))
@@ -58,9 +93,13 @@
     def load(c):
         return pltpu.make_async_copy(state_hbm.at[pl.ds(c * CHUNK, CHUNK)], raw.at[c], in_sem.at[c])
 
+    def load_force(c):
+        return pltpu.make_async_copy(force_hbm.at[pl.ds(c * CHUNK, CHUNK)], force.at[c], force_sem.at[c])
+
     @pl.loop(0, chunks)
     def _(c):
         load(c).start()
+        load_force(c).start()
 
     barrier = pltpu.get_barrier_semaphore()
     for place in [east, west] + far:
@@ -150,7 +189,7 @@
     first_row = (lat * rows).astype(jnp.float32)
 
     def advance(step, c, put):
-        pushes = jnp.swapaxes(force_ref[pl.ds(c * CHUNK, CHUNK)].astype(jnp.float32), 0, 1)
+        pushes = jnp.swapaxes(force[c].astype(jnp.float32), 0, 1)
         from_west = cols_in[step, 0, c]
         from_east = cols_in[step, 1, c]
         for r in range(rows):
@@ -178,6 +217,7 @@
     @pl.loop(0, chunks)
     def _(c):
         receive(0, c)
+        load_force(c).wait()
 
         def put(r, *new):
             for f in range(3):
@@ -187,8 +227,8 @@
         send(1, c)
 
     for r in range(rows):
-        cell = lax.broadcasted_iota(jnp.int32, (width, LANES), 0) + r * width
-        onehot[r] = jnp.where(cell == index_ref[0:1, :], 1.0, 0.0).astype(jnp.bfloat16)
+        cell = lax.broadcasted_iota(jnp.int32, (width, sites), 0) + r * width
+        onehot[r] = jnp.where(cell == index_ref[0], 1.0, 0.0).astype(jnp.bfloat16)
 
     def save(c):
         return pltpu.make_async_copy(fore.at[c], fore_hbm.at[c], out_sem.at[c])
@@ -203,20 +243,20 @@
 
         advance(1, c, put)
         save(c).start()
-        seen = jnp.zeros((CHUNK, LANES), jnp.float32)
+        seen = jnp.zeros((CHUNK, sites), jnp.float32)
         for r in range(rows):
             picked = jnp.dot(jnp.concatenate(parts_of(fore[c, 0, r], 3), axis=0), onehot[r],
                              preferred_element_type=jnp.float32)
             seen += (picked[:CHUNK] + picked[CHUNK:2 * CHUNK]) + picked[2 * CHUNK:]
         readings[c] = seen
 
-    seen = readings[...].reshape(members, LANES)
+    seen = readings[...].reshape(members, sites)
     mean = jnp.mean(seen, axis=0, keepdims=True)
     spread = seen - mean
-    inv = 1.0 / error_ref[0:1, :]
-    innovation = inv * (value_ref[0:1, :] - mean)
-    left = jnp.concatenate([spread * inv, jnp.broadcast_to(innovation, (8, LANES))], axis=0)
-    acc[0] = product(left, spread.T)
+    inv = 1.0 / error_ref[0]
+    innovation = inv * (value_ref[0] - mean)
+    left = jnp.concatenate([spread * inv, jnp.broadcast_to(innovation, (8, sites))], axis=0)
+    acc[0] = fold(product(left, spread.T))
     swaps = [pltpu.make_async_remote_copy(
         src_ref=acc.at[s], dst_ref=acc_in.at[s], send_sem=sum_send.at[s], recv_sem=sum_recv.at[s],
         device_id=dev(place), device_id_type=MESH) for s, place in enumerate(partners)]
@@ -246,6 +286,7 @@
 
 def analysis_kernel(sums_ref, fore_ref, out_ref, mix):
     members = sums_ref.shape[1]
+    half = members // 2
     rows = fore_ref.shape[2]
     width = fore_ref.shape[4]
 
@@ -253,18 +294,23 @@
     def _():
         eye = (lax.broadcasted_iota(jnp.int32, (members, members), 0)
                == lax.broadcasted_iota(jnp.int32, (members, members), 1)).astype(jnp.float32)
-        amat = (members - 1) * eye + sums_ref[:members]
+        amat = (members - 1) * eye + unfold(sums_ref[...])
         scale = jnp.sqrt(jnp.sum(jnp.sum(amat * amat, axis=1, keepdims=True), axis=0, keepdims=True))
 
         def turn(_, pair):
             upper, lower = pair
-            factor = 1.5 * eye - 0.5 * product(lower, upper)
-            return product(upper, factor), product(factor, lower)
-
-        _, lower = lax.fori_loop(0, NS_ITERS, turn, (amat / scale, eye))
+            factor = 1.5 * eye - 0.5 * paired(lower, upper)
+            both = paired(jnp.concatenate([upper, lower], axis=0), factor)
+            return both[:members], both[members:]
+
+        upper = amat / scale
+        lower = 1.5 * eye - 0.5 * upper
+        upper = paired(upper, lower)
+        upper, lower = lax.fori_loop(1, NS_ITERS - 1, turn, (upper, lower))
+        lower = paired(lower, 1.5 * eye - 0.5 * paired(lower, upper))
         root = lower / jnp.sqrt(scale)
-        inverse = product(root, root)
-        shift = product(sums_ref[members:], inverse.T)
+        inverse = paired(root, root)
+        shift = paired(sums_ref[half:], inverse.T)
         weights = math.sqrt(members - 1) * root.T + shift[0:1, :]
         high = weights.astype(jnp.bfloat16)
         low = (weights - high.astype(jnp.float32)).astype(jnp.bfloat16)
@@ -286,11 +332,7 @@
 def shards(n_lat, n_lon, ocean_status, height_driver, obs_index, obs_value, obs_error):
     members, fields, rows, width = ocean_status.shape
     chunks = members // CHUNK
-    spare = LANES - obs_index.shape[-1]
-
-    def flat(array, fill):
-        return jnp.pad(array.reshape(1, -1), ((0, 0), (0, spare)), constant_values=fill)
-
+    sites = obs_index.shape[-1]
     vmem = pl.BlockSpec(memory_space=pltpu.VMEM)
     anywhere = pl.BlockSpec(memory_space=pl.ANY)
     stages = len(doublings(n_lon)) + len(doublings(n_lat))
@@ -299,36 +341,37 @@
     block = (chunks, fields, rows, CHUNK, width)
     fore, sums = pl.pallas_call(
         functools.partial(forecast_kernel, n_lat, n_lon),
-        out_shape=(jax.ShapeDtypeStruct(block, f32), jax.ShapeDtypeStruct((members + 8, members), f32)),
-        in_specs=[anywhere, vmem, vmem, vmem, vmem],
+        out_shape=(jax.ShapeDtypeStruct(block, f32), jax.ShapeDtypeStruct((members // 2 + 8, members), f32)),
+        in_specs=[anywhere, anywhere, vmem, vmem, vmem],
         out_specs=(anywhere, vmem),
         scratch_shapes=[
             pltpu.VMEM((chunks, CHUNK, fields, rows, width), f32),
+            pltpu.VMEM((chunks, CHUNK, rows, width), height_driver.dtype),
             pltpu.VMEM((2, chunks, fields, rows + 2, CHUNK, width), f32),
             pltpu.VMEM((2, 2, chunks, CHUNK, LANES), f32),
             pltpu.VMEM((2, 2, chunks, CHUNK, LANES), f32),
             pltpu.VMEM(block, f32),
-            pltpu.VMEM((rows, width, LANES), jnp.bfloat16),
-            pltpu.VMEM((chunks, CHUNK, LANES), f32),
-            pltpu.VMEM((stages + 1, members + 8, members), f32),
-            pltpu.VMEM((stages, members + 8, members), f32),
-            dma((chunks,)), dma((chunks,)),
+            pltpu.VMEM((rows, width, sites), jnp.bfloat16),
+            pltpu.VMEM((chunks, CHUNK, sites), f32),
+            pltpu.VMEM((stages + 1, members // 2 + 8, members), f32),
+            pltpu.VMEM((stages, members // 2 + 8, members), f32),
+            dma((chunks,)), dma((chunks,)), dma((chunks,)),
             dma((2, 2, chunks)), dma((2, 2, chunks)),
             dma((2, 2, chunks)), dma((2, 2, chunks)),
             dma((stages,)), dma((stages,)),
         ],
-        compiler_params=pltpu.CompilerParams(collective_id=0, has_side_effects=True, vmem_limit_bytes=52 << 20),
+        compiler_params=pltpu.CompilerParams(collective_id=0, has_side_effects=True, vmem_limit_bytes=63 << 20),
         name="forecast",
-    )(ocean_status, height_driver, flat(obs_index, -1), flat(obs_value, 0), flat(obs_error, 1))
+    )(ocean_status, height_driver, obs_index, obs_value, obs_error)
     return pl.pallas_call(
         analysis_kernel,
         grid=(fields,),
         out_shape=jax.ShapeDtypeStruct(ocean_status.shape, f32),
-        in_specs=[pl.BlockSpec((members + 8, members), lambda i: (0, 0)),
+        in_specs=[pl.BlockSpec((members // 2 + 8, members), lambda i: (0, 0)),
                   pl.BlockSpec((chunks, 1, rows, CHUNK, width), lambda i: (0, i, 0, 0, 0))],
         out_specs=pl.BlockSpec((members, 1, rows, width), lambda i: (0, i, 0, 0)),
         scratch_shapes=[pltpu.VMEM((2 * members, 2 * members), jnp.bfloat16)],
-        compiler_params=pltpu.CompilerParams(vmem_limit_bytes=48 << 20),
+        compiler_params=pltpu.CompilerParams(vmem_limit_bytes=63 << 20),
         name="analysis",
     )(sums, fore)
 

time: 109 us -> 104 us (0.954)
  local copies, waits for them, and re-layouts: 3.2 us -> 0 us
  Pallas kernels: 105 us -> 103 us
    pad x3 -> x0, local copies, waits for them, and re-layouts: 1.98 us -> none  [flat(): jnp.pad(array.reshape(1, -1), ((0, 0), (0, spare)), constant_values=fill)]
    pallas_call x1, Pallas kernels: 90.9 us -> 89.6 us  [shards(): pl.pallas_call(functools.partial(forecast_kernel, n_lat, n_lon), out_shap...]
    unnamed x2 -> x0, local copies, waits for them, and re-layouts: 1.22 us -> none
where the time goes in v2:
time: 104 us; the launch traced here: 103 us
  Pallas kernels  103 us (99%)
    pallas_call x1, Pallas kernels, shards(): pl.pallas_call(functools.partial(forecast_kernel, n_lat, n_lon), out_shap...  89.6 us
    pallas_call x1, Pallas kernels, shards(): pl.pallas_call(analysis_kernel, grid=(fields,), out_shape=jax.ShapeDtypeS...  13.8 us

profile of v2, /device:TPU:0, one launch (start us, length us, event | category | flops | bytes accessed | tf_op | source)
XLA Modules:
  0.0 103.5 jit_solution(7579883379456566092)
XLA Ops:
  0.0 89.6 %forecast.1 = (f32[8,3,8,16,512]{4,3,2,1,0:T(8,128)}, f32[72,128]{1,0:T(8,128)}) custom-call(f32[128,3,8,512]{3,2,1,0:T(8,128)} %state_hbm.1, bf16[128,8,512]{2,1,0:T(8,128)(2,1)} %force_hbm.1, s32[1,1,64]{2,1,0:T(1,128)} %index_ref.1, f32[1,1,64]{2,1,0:T(1,128)} %value_ref.1, f32[1,1,64]{2,1,0:T(1,128)} %error_ref.1), custom_call_target="tpu_custom_call" | custom-call | tf_op jit(solution)/shard_map/forecast/pallas_call | solution.py:342
  89.6 13.8 %analysis.1 = f32[128,3,8,512]{3,2,1,0:T(8,128)} custom-call(f32[72,128]{1,0:T(8,128)} %get-tuple-element.7.sums_ref, f32[8,3,8,16,512]{4,3,2,1,0:T(8,128)} %get-tuple-element.8.fore_ref), custom_call_target="tpu_custom_call" | custom-call | tf_op jit(solution)/shard_map/analysis/pallas_call | solution.py:366

commit v3 on v2

--- a/solution.py
+++ b/solution.py
@@ -72,8 +72,8 @@
 
 
 def forecast_kernel(n_lat, n_lon, state_hbm, force_hbm, index_ref, value_ref, error_ref, fore_hbm, sums_ref,
-                    raw, force, ext, cols_out, cols_in, fore, onehot, readings, acc, acc_in,
-                    in_sem, force_sem, out_sem, row_send, row_recv, col_send, col_recv, sum_send, sum_recv):
+                    raw, force, ext, relay, cols_out, cols_in, fore, onehot, readings, acc, acc_in,
+                    in_sem, force_sem, out_sem, row_send, row_recv, relay_recv, relay_send, col_send, col_recv, sum_send, sum_recv):
     chunks = raw.shape[0]
     members = chunks * CHUNK
     sites = index_ref.shape[-1]
@@ -84,6 +84,15 @@
     has_south, has_north = lat > 0, lat < n_lat - 1
     south, north = (jnp.maximum(lat - 1, 0), lon), (jnp.minimum(lat + 1, n_lat - 1), lon)
 
+    planes = n_lat // 2
+    parity = lax.rem(lat, 2)
+    plane = lat // 2
+    detours_out = chunks * (parity * (planes - 1 - plane) + (1 - parity) * plane) // planes
+    detours_by = chunks * ((1 - parity) * (planes - 1 - plane) + parity * plane) // planes
+
+    def detoured(c, count):
+        return lax.rem((chunks - 1 - c) * count, chunks) >= chunks - count
+
     def dev(place):
         return {"lat": place[0], "lon": place[1]}
 
@@ -113,7 +122,16 @@
     def _():
         pl.semaphore_signal(barrier, inc=1, device_id=dev(north), device_id_type=MESH)
 
-    pl.semaphore_wait(barrier, 2 + len(far) + has_south.astype(jnp.int32) + has_north.astype(jnp.int32))
+    @pl.when(lat > 1)
+    def _():
+        pl.semaphore_signal(barrier, inc=1, device_id=dev((jnp.maximum(lat - 2, 0), lon)), device_id_type=MESH)
+
+    @pl.when(lat < n_lat - 2)
+    def _():
+        pl.semaphore_signal(barrier, inc=1, device_id=dev((jnp.minimum(lat + 2, n_lat - 1), lon)), device_id_type=MESH)
+
+    present = [has_south, has_north, lat > 1, lat < n_lat - 2]
+    pl.semaphore_wait(barrier, 2 + len(far) + sum(there.astype(jnp.int32) for there in present))
 
     def row_copy(step, c, side):
         return pltpu.make_async_remote_copy(
@@ -122,6 +140,24 @@
             send_sem=row_send.at[step, side, c], recv_sem=row_recv.at[step, side, c],
             device_id=dev(north if side == 0 else south), device_id_type=MESH)
 
+    def detour_copy(step, c):
+        return pltpu.make_async_remote_copy(
+            src_ref=ext.at[step, c, :, 1 + (rows - 1) * parity], dst_ref=relay.at[step, c],
+            send_sem=row_send.at[step, 1 - parity, c], recv_sem=relay_recv.at[step, c],
+            device_id=dev((lat + 1 - 2 * parity, lon)), device_id_type=MESH)
+
+    def onward_copy(step, c):
+        return pltpu.make_async_remote_copy(
+            src_ref=relay.at[step, c], dst_ref=ext.at[step, c, :, (rows + 1) * parity],
+            send_sem=relay_send.at[step, c], recv_sem=row_recv.at[step, parity, c],
+            device_id=dev((jnp.clip(lat + 2 - 4 * parity, 0, n_lat - 1), lon)), device_id_type=MESH)
+
+    def hand_on(step, c):
+        @pl.when(detoured(c, detours_by))
+        def _():
+            detour_copy(step, c).wait_recv()
+            onward_copy(step, c).start()
+
     def col_copy(step, c, side):
         return pltpu.make_async_remote_copy(
             src_ref=cols_out.at[step, side, c], dst_ref=cols_in.at[step, side, c],
@@ -132,11 +168,17 @@
     wide = lax.broadcasted_iota(jnp.int32, (CHUNK, width), 1)
 
     def send(step, c):
-        @pl.when(has_north)
+        by = detoured(c, detours_out)
+
+        @pl.when(by)
+        def _():
+            detour_copy(step, c).start()
+
+        @pl.when(has_north & jnp.logical_not(by & (parity == 1)))
         def _():
             row_copy(step, c, 0).start()
 
-        @pl.when(has_south)
+        @pl.when(has_south & jnp.logical_not(by & (parity == 0)))
         def _():
             row_copy(step, c, 1).start()
 
@@ -216,6 +258,7 @@
 
     @pl.loop(0, chunks)
     def _(c):
+        hand_on(0, c)
         receive(0, c)
         load_force(c).wait()
 
@@ -235,6 +278,7 @@
 
     @pl.loop(0, chunks)
     def _(c):
+        hand_on(1, c)
         receive(1, c)
 
         def put(r, *new):
@@ -279,6 +323,10 @@
             @pl.when(has_south)
             def _():
                 row_copy(step, c, 1).wait_send()
+
+            @pl.when(detoured(c, detours_by))
+            def _():
+                onward_copy(step, c).wait_send()
 
             col_copy(step, c, 0).wait_send()
             col_copy(step, c, 1).wait_send()
@@ -348,6 +396,7 @@
             pltpu.VMEM((chunks, CHUNK, fields, rows, width), f32),
             pltpu.VMEM((chunks, CHUNK, rows, width), height_driver.dtype),
             pltpu.VMEM((2, chunks, fields, rows + 2, CHUNK, width), f32),
+            pltpu.VMEM((2, chunks, fields, CHUNK, width), f32),
             pltpu.VMEM((2, 2, chunks, CHUNK, LANES), f32),
             pltpu.VMEM((2, 2, chunks, CHUNK, LANES), f32),
             pltpu.VMEM(block, f32),
@@ -357,6 +406,7 @@
             pltpu.VMEM((stages, members // 2 + 8, members), f32),
             dma((chunks,)), dma((chunks,)), dma((chunks,)),
             dma((2, 2, chunks)), dma((2, 2, chunks)),
+            dma((2, chunks)), dma((2, chunks)),
             dma((2, 2, chunks)), dma((2, 2, chunks)),
             dma((stages,)), dma((stages,)),
         ],

time: 104 us -> 96.9 us (0.932)
  Pallas kernels: 103 us -> 96.7 us
    pallas_call x1, Pallas kernels: 89.6 us -> 82.9 us  [shards(): pl.pallas_call(functools.partial(forecast_kernel, n_lat, n_lon), out_shap...]
where the time goes in v3:
time: 96.9 us; the launch traced here: 96.8 us
  Pallas kernels  96.7 us (100%)
    pallas_call x1, Pallas kernels, shards(): pl.pallas_call(functools.partial(forecast_kernel, n_lat, n_lon), out_shap...  82.9 us
    pallas_call x1, Pallas kernels, shards(): pl.pallas_call(analysis_kernel, grid=(fields,), out_shape=jax.ShapeDtypeS...  13.8 us

profile of v3, /device:TPU:0, one launch (start us, length us, event | category | flops | bytes accessed | tf_op | source)
XLA Modules:
  0.0 96.8 jit_solution(3485814304188859655)
XLA Ops:
  0.0 82.9 %forecast.1 = (f32[8,3,8,16,512]{4,3,2,1,0:T(8,128)}, f32[72,128]{1,0:T(8,128)}) custom-call(f32[128,3,8,512]{3,2,1,0:T(8,128)} %state_hbm.1, bf16[128,8,512]{2,1,0:T(8,128)(2,1)} %force_hbm.1, s32[1,1,64]{2,1,0:T(1,128)} %index_ref.1, f32[1,1,64]{2,1,0:T(1,128)} %value_ref.1, f32[1,1,64]{2,1,0:T(1,128)} %error_ref.1), custom_call_target="tpu_custom_call" | custom-call | tf_op jit(solution)/shard_map/forecast/pallas_call | solution.py:390
  82.9 13.8 %analysis.1 = f32[128,3,8,512]{3,2,1,0:T(8,128)} custom-call(f32[72,128]{1,0:T(8,128)} %get-tuple-element.7.sums_ref, f32[8,3,8,16,512]{4,3,2,1,0:T(8,128)} %get-tuple-element.8.fore_ref), custom_call_target="tpu_custom_call" | custom-call | tf_op jit(solution)/shard_map/analysis/pallas_call | solution.py:416

commit v4 on v3

--- a/solution.py
+++ b/solution.py
@@ -71,8 +71,8 @@
     return jnp.where(row < half, first, last)
 
 
-def forecast_kernel(n_lat, n_lon, state_hbm, force_hbm, index_ref, value_ref, error_ref, fore_hbm, sums_ref,
-                    raw, force, ext, relay, cols_out, cols_in, fore, onehot, readings, acc, acc_in,
+def forecast_kernel(n_lat, n_lon, state_hbm, force_hbm, index_ref, value_ref, error_ref, terms_hbm, mean_ref, sums_ref,
+                    raw, force, ext, relay, cols_out, cols_in, fore, terms, onehot, readings, acc, acc_in,
                     in_sem, force_sem, out_sem, row_send, row_recv, relay_recv, relay_send, col_send, col_recv, sum_send, sum_recv):
     chunks = raw.shape[0]
     members = chunks * CHUNK
@@ -273,8 +273,8 @@
         cell = lax.broadcasted_iota(jnp.int32, (width, sites), 0) + r * width
         onehot[r] = jnp.where(cell == index_ref[0], 1.0, 0.0).astype(jnp.bfloat16)
 
-    def save(c):
-        return pltpu.make_async_copy(fore.at[c], fore_hbm.at[c], out_sem.at[c])
+    def save(i):
+        return pltpu.make_async_copy(terms.at[i], terms_hbm.at[i], out_sem.at[i])
 
     @pl.loop(0, chunks)
     def _(c):
@@ -286,7 +286,6 @@
                 fore[c, f, r] = new[f]
 
         advance(1, c, put)
-        save(c).start()
         seen = jnp.zeros((CHUNK, sites), jnp.float32)
         for r in range(rows):
             picked = jnp.dot(jnp.concatenate(parts_of(fore[c, 0, r], 3), axis=0), onehot[r],
@@ -304,8 +303,18 @@
     swaps = [pltpu.make_async_remote_copy(
         src_ref=acc.at[s], dst_ref=acc_in.at[s], send_sem=sum_send.at[s], recv_sem=sum_recv.at[s],
         device_id=dev(place), device_id_type=MESH) for s, place in enumerate(partners)]
+    items = 3 * rows
     for s, swap in enumerate(swaps):
         swap.start()
+
+        @pl.loop(s * items // len(swaps), (s + 1) * items // len(swaps))
+        def _(i):
+            cells = fore[:, i // rows, lax.rem(i, rows)].reshape(members, width)
+            mean = jnp.mean(cells, axis=0, keepdims=True)
+            terms[i] = jnp.concatenate(parts_of(cells - mean, 2), axis=0)
+            mean_ref[i] = mean
+            save(i).start()
+
         swap.wait_recv()
         acc[s + 1] = acc[s] + acc_in[s]
     sums_ref[...] = acc[len(swaps)]
@@ -314,7 +323,6 @@
 
     @pl.loop(0, chunks)
     def _(c):
-        save(c).wait()
         for step in range(2):
             @pl.when(has_north)
             def _():
@@ -331,12 +339,15 @@
             col_copy(step, c, 0).wait_send()
             col_copy(step, c, 1).wait_send()
 
-
-def analysis_kernel(sums_ref, fore_ref, out_ref, mix):
+    @pl.loop(0, items)
+    def _(i):
+        save(i).wait()
+
+
+def analysis_kernel(sums_ref, terms_ref, mean_ref, out_ref, mix, moved):
     members = sums_ref.shape[1]
     half = members // 2
-    rows = fore_ref.shape[2]
-    width = fore_ref.shape[4]
+    rows = terms_ref.shape[0]
 
     @pl.when(pl.program_id(0) == 0)
     def _():
@@ -368,13 +379,10 @@
         mix[members:, members:] = jnp.zeros_like(low)
 
     for r in range(rows):
-        cells = fore_ref[:, 0, r].reshape(members, width)
-        mean = jnp.mean(cells, axis=0, keepdims=True)
-        spread = cells - mean
-        high = spread.astype(jnp.bfloat16)
-        low = (spread - high.astype(jnp.float32)).astype(jnp.bfloat16)
-        both = jnp.dot(mix[...], jnp.concatenate([high, low], axis=0), preferred_element_type=jnp.float32)
-        out_ref[:, 0, r, :] = mean + both[:members] + both[members:]
+        both = jnp.dot(mix[...], terms_ref[r], preferred_element_type=jnp.float32)
+        moved[r] = mean_ref[r] + both[:members] + both[members:]
+    for m in range(0, members, CHUNK):
+        out_ref[m:m + CHUNK, 0] = jnp.swapaxes(moved[:, m:m + CHUNK], 0, 1)
 
 
 def shards(n_lat, n_lon, ocean_status, height_driver, obs_index, obs_value, obs_error):
@@ -387,11 +395,13 @@
     dma = pltpu.SemaphoreType.DMA
     f32 = jnp.float32
     block = (chunks, fields, rows, CHUNK, width)
-    fore, sums = pl.pallas_call(
+    terms, mean, sums = pl.pallas_call(
         functools.partial(forecast_kernel, n_lat, n_lon),
-        out_shape=(jax.ShapeDtypeStruct(block, f32), jax.ShapeDtypeStruct((members // 2 + 8, members), f32)),
+        out_shape=(jax.ShapeDtypeStruct((fields * rows, 2 * members, width), jnp.bfloat16),
+                   jax.ShapeDtypeStruct((fields * rows, 1, width), f32),
+                   jax.ShapeDtypeStruct((members // 2 + 8, members), f32)),
         in_specs=[anywhere, anywhere, vmem, vmem, vmem],
-        out_specs=(anywhere, vmem),
+        out_specs=(anywhere, vmem, vmem),
         scratch_shapes=[
             pltpu.VMEM((chunks, CHUNK, fields, rows, width), f32),
             pltpu.VMEM((chunks, CHUNK, rows, width), height_driver.dtype),
@@ -400,11 +410,12 @@
             pltpu.VMEM((2, 2, chunks, CHUNK, LANES), f32),
             pltpu.VMEM((2, 2, chunks, CHUNK, LANES), f32),
             pltpu.VMEM(block, f32),
+            pltpu.VMEM((fields * rows, 2 * members, width), jnp.bfloat16),
             pltpu.VMEM((rows, width, sites), jnp.bfloat16),
             pltpu.VMEM((chunks, CHUNK, sites), f32),
             pltpu.VMEM((stages + 1, members // 2 + 8, members), f32),
             pltpu.VMEM((stages, members // 2 + 8, members), f32),
-            dma((chunks,)), dma((chunks,)), dma((chunks,)),
+            dma((chunks,)), dma((chunks,)), dma((fields * rows,)),
             dma((2, 2, chunks)), dma((2, 2, chunks)),
             dma((2, chunks)), dma((2, chunks)),
             dma((2, 2, chunks)), dma((2, 2, chunks)),
@@ -418,12 +429,14 @@
         grid=(fields,),
         out_shape=jax.ShapeDtypeStruct(ocean_status.shape, f32),
         in_specs=[pl.BlockSpec((members // 2 + 8, members), lambda i: (0, 0)),
-                  pl.BlockSpec((chunks, 1, rows, CHUNK, width), lambda i: (0, i, 0, 0, 0))],
+                  pl.BlockSpec((rows, 2 * members, width), lambda i: (i, 0, 0)),
+                  pl.BlockSpec((rows, 1, width), lambda i: (i, 0, 0))],
         out_specs=pl.BlockSpec((members, 1, rows, width), lambda i: (0, i, 0, 0)),
-        scratch_shapes=[pltpu.VMEM((2 * members, 2 * members), jnp.bfloat16)],
+        scratch_shapes=[pltpu.VMEM((2 * members, 2 * members), jnp.bfloat16),
+                        pltpu.VMEM((rows, members, width), f32)],
         compiler_params=pltpu.CompilerParams(vmem_limit_bytes=63 << 20),
         name="analysis",
-    )(sums, fore)
+    )(sums, terms, mean)
 
 
 def solution(mesh):

time: 96.9 us -> 97.4 us (level)
  no operation moved by 1% of the time
where the time goes in v4:
time: 97.4 us; the launch traced here: 97.2 us
  Pallas kernels  97.2 us (100%)
    pallas_call x1, Pallas kernels, shards(): pl.pallas_call(functools.partial(forecast_kernel, n_lat, n_lon), out_shap...  83.3 us
    pallas_call x1, Pallas kernels, shards(): pl.pallas_call(analysis_kernel, grid=(fields,), out_shape=jax.ShapeDtypeS...  13.9 us

profile of v4, /device:TPU:0, one launch (start us, length us, event | category | flops | bytes accessed | tf_op | source)
XLA Modules:
  0.0 97.2 jit_solution(9983496439747834216)
XLA Ops:
  0.0 83.3 %forecast.1 = (bf16[24,256,512]{2,1,0:T(8,128)(2,1)}, f32[24,1,512]{2,1,0:T(1,128)}, f32[72,128]{1,0:T(8,128)}) custom-call(f32[128,3,8,512]{3,2,1,0:T(8,128)} %state_hbm.1, bf16[128,8,512]{2,1,0:T(8,128)(2,1)} %force_hbm.1, s32[1,1,64]{2,1,0:T(1,128)} %index_ref.1, f32[1,1,64]{2,1,0:T(1,128)} %value_ref.1, f32[1,1,64]{2,1,0:T(1,128)} %error_ref.1), custom_call_target="tpu_custom_call" | custom-call | tf_op jit(solution)/shard_map/forecast/pallas_call | solution.py:398
  83.3 13.9 %analysis.1 = f32[128,3,8,512]{3,2,1,0:T(8,128)} custom-call(f32[72,128]{1,0:T(8,128)} %get-tuple-element.8.sums_ref, bf16[24,256,512]{2,1,0:T(8,128)(2,1)} %get-tuple-element.9.terms_ref, f32[24,1,512]{2,1,0:T(1,128)} %get-tuple-element.10.mean_ref), custom_call_target="tpu_custom_call" | custom-call | tf_op jit(solution)/shard_map/analysis/pallas_call | solution.py:427

commit v5 on v4

--- a/solution.py
+++ b/solution.py
@@ -13,7 +13,8 @@
 DIFFUSION = 0.1
 FORCE_STEP = 0.5
 CORIOLIS_MAX = 0.3
-CHUNK = 16
+CHUNK = 8
+LAG = 3
 LANES = 128
 MESH = pl.DeviceIdType.MESH
 
@@ -130,6 +131,24 @@
     def _():
         pl.semaphore_signal(barrier, inc=1, device_id=dev((jnp.minimum(lat + 2, n_lat - 1), lon)), device_id_type=MESH)
 
+    for r in range(rows):
+        cell = lax.broadcasted_iota(jnp.int32, (width, sites), 0) + r * width
+        onehot[r] = jnp.where(cell == index_ref[0], 1.0, 0.0).astype(jnp.bfloat16)
+
+    @pl.when(lat == 0)
+    def _():
+        for step in range(2):
+            @pl.loop(0, chunks)
+            def _(c):
+                ext[step, c, :, 0] = jnp.zeros((3, CHUNK, width), jnp.float32)
+
+    @pl.when(lat == n_lat - 1)
+    def _():
+        for step in range(2):
+            @pl.loop(0, chunks)
+            def _(c):
+                ext[step, c, :, rows + 1] = jnp.zeros((3, CHUNK, width), jnp.float32)
+
     present = [has_south, has_north, lat > 1, lat < n_lat - 2]
     pl.semaphore_wait(barrier, 2 + len(far) + sum(there.astype(jnp.int32) for there in present))
 
@@ -206,27 +225,6 @@
         col_copy(step, c, 0).wait_recv()
         col_copy(step, c, 1).wait_recv()
 
-    @pl.when(lat == 0)
-    def _():
-        for step in range(2):
-            @pl.loop(0, chunks)
-            def _(c):
-                ext[step, c, :, 0] = jnp.zeros((3, CHUNK, width), jnp.float32)
-
-    @pl.when(lat == n_lat - 1)
-    def _():
-        for step in range(2):
-            @pl.loop(0, chunks)
-            def _(c):
-                ext[step, c, :, rows + 1] = jnp.zeros((3, CHUNK, width), jnp.float32)
-
-    @pl.loop(0, chunks)
-    def _(c):
-        load(c).wait()
-        for f in range(3):
-            ext[0, c, f, pl.ds(1, rows)] = jnp.swapaxes(raw[c, :, f], 0, 1)
-        send(0, c)
-
     total_rows = float(n_lat * rows)
     first_row = (lat * rows).astype(jnp.float32)
 
@@ -256,8 +254,16 @@
                      - COURANT * coriolis * u + DIFFUSION * (ve + vw + vn + vs - 4.0 * v))
             put(r, h_new, u_new, v_new)
 
-    @pl.loop(0, chunks)
-    def _(c):
+    def save(i):
+        return pltpu.make_async_copy(terms.at[i], terms_hbm.at[i], out_sem.at[i])
+
+    def begin(c):
+        load(c).wait()
+        for f in range(3):
+            ext[0, c, f, pl.ds(1, rows)] = jnp.swapaxes(raw[c, :, f], 0, 1)
+        send(0, c)
+
+    def first_step(c):
         hand_on(0, c)
         receive(0, c)
         load_force(c).wait()
@@ -269,15 +275,7 @@
         advance(0, c, put)
         send(1, c)
 
-    for r in range(rows):
-        cell = lax.broadcasted_iota(jnp.int32, (width, sites), 0) + r * width
-        onehot[r] = jnp.where(cell == index_ref[0], 1.0, 0.0).astype(jnp.bfloat16)
-
-    def save(i):
-        return pltpu.make_async_copy(terms.at[i], terms_hbm.at[i], out_sem.at[i])
-
-    @pl.loop(0, chunks)
-    def _(c):
+    def second_step(c):
         hand_on(1, c)
         receive(1, c)
 
@@ -288,10 +286,25 @@
         advance(1, c, put)
         seen = jnp.zeros((CHUNK, sites), jnp.float32)
         for r in range(rows):
-            picked = jnp.dot(jnp.concatenate(parts_of(fore[c, 0, r], 3), axis=0), onehot[r],
+            terms_here = [part.astype(jnp.float32) for part in parts_of(fore[c, 0, r], 3)]
+            picked = jnp.dot(jnp.concatenate(terms_here, axis=0).astype(jnp.bfloat16), onehot[r],
                              preferred_element_type=jnp.float32)
             seen += (picked[:CHUNK] + picked[CHUNK:2 * CHUNK]) + picked[2 * CHUNK:]
         readings[c] = seen
+
+    @pl.loop(0, chunks + 2 * LAG)
+    def _(t):
+        @pl.when(t < chunks)
+        def _():
+            begin(t)
+
+        @pl.when((t >= LAG) & (t < chunks + LAG))
+        def _():
+            first_step(t - LAG)
+
+        @pl.when(t >= 2 * LAG)
+        def _():
+            second_step(t - 2 * LAG)
 
     seen = readings[...].reshape(members, sites)
     mean = jnp.mean(seen, axis=0, keepdims=True)
@@ -359,14 +372,13 @@
         def turn(_, pair):
             upper, lower = pair
             factor = 1.5 * eye - 0.5 * paired(lower, upper)
-            both = paired(jnp.concatenate([upper, lower], axis=0), factor)
-            return both[:members], both[members:]
+            return paired(factor, upper), paired(factor, lower)
 
         upper = amat / scale
         lower = 1.5 * eye - 0.5 * upper
-        upper = paired(upper, lower)
-        upper, lower = lax.fori_loop(1, NS_ITERS - 1, turn, (upper, lower))
-        lower = paired(lower, 1.5 * eye - 0.5 * paired(lower, upper))
+        upper = paired(lower, upper)
+        upper, lower = lax.fori_loop(1, NS_ITERS - 1, turn, (upper, lower), unroll=True)
+        lower = paired(1.5 * eye - 0.5 * paired(lower, upper), lower)
         root = lower / jnp.sqrt(scale)
         inverse = paired(root, root)
         shift = paired(sums_ref[half:], inverse.T)

time: 97.4 us -> 101 us (1.037)
  Pallas kernels: 97.2 us -> 101 us
    pallas_call x1, Pallas kernels: 83.3 us -> 88.1 us  [shards(): pl.pallas_call(functools.partial(forecast_kernel, n_lat, n_lon), out_shap...]
where the time goes in v5:
time: 101 us
  Pallas kernels  101 us (100%)
    pallas_call x1, Pallas kernels, shards(): pl.pallas_call(functools.partial(forecast_kernel, n_lat, n_lon), out_shap...  88.1 us
    pallas_call x1, Pallas kernels, shards(): pl.pallas_call(analysis_kernel, grid=(fields,), out_shape=jax.ShapeDtypeS...  13 us

profile of v5, /device:TPU:0, one launch (start us, length us, event | category | flops | bytes accessed | tf_op | source)
XLA Modules:
  0.0 101.1 jit_solution(17052072854739025939)
XLA Ops:
  0.0 88.1 %forecast.1 = (bf16[24,256,512]{2,1,0:T(8,128)(2,1)}, f32[24,1,512]{2,1,0:T(1,128)}, f32[72,128]{1,0:T(8,128)}) custom-call(f32[128,3,8,512]{3,2,1,0:T(8,128)} %state_hbm.1, bf16[128,8,512]{2,1,0:T(8,128)(2,1)} %force_hbm.1, s32[1,1,64]{2,1,0:T(1,128)} %index_ref.1, f32[1,1,64]{2,1,0:T(1,128)} %value_ref.1, f32[1,1,64]{2,1,0:T(1,128)} %error_ref.1), custom_call_target="tpu_custom_call" | custom-call | tf_op jit(solution)/shard_map/forecast/pallas_call | solution.py:410
  88.1 13.0 %analysis.1 = f32[128,3,8,512]{3,2,1,0:T(8,128)} custom-call(f32[72,128]{1,0:T(8,128)} %get-tuple-element.8.sums_ref, bf16[24,256,512]{2,1,0:T(8,128)(2,1)} %get-tuple-element.9.terms_ref, f32[24,1,512]{2,1,0:T(1,128)} %get-tuple-element.10.mean_ref), custom_call_target="tpu_custom_call" | custom-call | tf_op jit(solution)/shard_map/analysis/pallas_call | solution.py:439

commit v6 on v5

--- a/solution.py
+++ b/solution.py
@@ -13,8 +13,7 @@
 DIFFUSION = 0.1
 FORCE_STEP = 0.5
 CORIOLIS_MAX = 0.3
-CHUNK = 8
-LAG = 3
+CHUNK = 16
 LANES = 128
 MESH = pl.DeviceIdType.MESH
 
@@ -73,7 +72,7 @@
 
 
 def forecast_kernel(n_lat, n_lon, state_hbm, force_hbm, index_ref, value_ref, error_ref, terms_hbm, mean_ref, sums_ref,
-                    raw, force, ext, relay, cols_out, cols_in, fore, terms, onehot, readings, acc, acc_in,
+                    raw, force, ext, relay, cols_out, cols_in, fore, terms, onehot, acc, acc_in,
                     in_sem, force_sem, out_sem, row_send, row_recv, relay_recv, relay_send, col_send, col_recv, sum_send, sum_recv):
     chunks = raw.shape[0]
     members = chunks * CHUNK
@@ -186,7 +185,7 @@
     lane = lax.broadcasted_iota(jnp.int32, (CHUNK, LANES), 1)
     wide = lax.broadcasted_iota(jnp.int32, (CHUNK, width), 1)
 
-    def send(step, c):
+    def send_rows(step, c):
         by = detoured(c, detours_out)
 
         @pl.when(by)
@@ -201,6 +200,7 @@
         def _():
             row_copy(step, c, 1).start()
 
+    def send_columns(step, c):
         last = jnp.zeros((CHUNK, LANES), jnp.float32)
         first = last
         for f in range(3):
@@ -232,7 +232,7 @@
         pushes = jnp.swapaxes(force[c].astype(jnp.float32), 0, 1)
         from_west = cols_in[step, 0, c]
         from_east = cols_in[step, 1, c]
-        for r in range(rows):
+        for r in [0, rows - 1] + list(range(1, rows - 1)):
             coriolis = CORIOLIS_MAX * (2.0 * (first_row + (r + 0.5)) / total_rows - 1.0)
 
             def around(f):
@@ -261,7 +261,8 @@
         load(c).wait()
         for f in range(3):
             ext[0, c, f, pl.ds(1, rows)] = jnp.swapaxes(raw[c, :, f], 0, 1)
-        send(0, c)
+        send_rows(0, c)
+        send_columns(0, c)
 
     def first_step(c):
         hand_on(0, c)
@@ -271,9 +272,11 @@
         def put(r, *new):
             for f in range(3):
                 ext[1, c, f, r + 1] = new[f]
+            if r == rows - 1:
+                send_rows(1, c)
 
         advance(0, c, put)
-        send(1, c)
+        send_columns(1, c)
 
     def second_step(c):
         hand_on(1, c)
@@ -284,29 +287,16 @@
                 fore[c, f, r] = new[f]
 
         advance(1, c, put)
-        seen = jnp.zeros((CHUNK, sites), jnp.float32)
-        for r in range(rows):
-            terms_here = [part.astype(jnp.float32) for part in parts_of(fore[c, 0, r], 3)]
-            picked = jnp.dot(jnp.concatenate(terms_here, axis=0).astype(jnp.bfloat16), onehot[r],
-                             preferred_element_type=jnp.float32)
-            seen += (picked[:CHUNK] + picked[CHUNK:2 * CHUNK]) + picked[2 * CHUNK:]
-        readings[c] = seen
-
-    @pl.loop(0, chunks + 2 * LAG)
-    def _(t):
-        @pl.when(t < chunks)
-        def _():
-            begin(t)
-
-        @pl.when((t >= LAG) & (t < chunks + LAG))
-        def _():
-            first_step(t - LAG)
-
-        @pl.when(t >= 2 * LAG)
-        def _():
-            second_step(t - 2 * LAG)
-
-    seen = readings[...].reshape(members, sites)
+
+    pl.loop(0, chunks)(begin)
+    pl.loop(0, chunks)(first_step)
+    pl.loop(0, chunks)(second_step)
+
+    seen = jnp.zeros((members, sites), jnp.float32)
+    for r in range(rows):
+        terms_here = parts_of(fore[:, 0, r].reshape(members, width), 3)
+        picked = jnp.dot(jnp.concatenate(terms_here, axis=0), onehot[r], preferred_element_type=jnp.float32)
+        seen += (picked[:members] + picked[members:2 * members]) + picked[2 * members:]
     mean = jnp.mean(seen, axis=0, keepdims=True)
     spread = seen - mean
     inv = 1.0 / error_ref[0]
@@ -424,7 +414,6 @@
             pltpu.VMEM(block, f32),
             pltpu.VMEM((fields * rows, 2 * members, width), jnp.bfloat16),
             pltpu.VMEM((rows, width, sites), jnp.bfloat16),
-            pltpu.VMEM((chunks, CHUNK, sites), f32),
             pltpu.VMEM((stages + 1, members // 2 + 8, members), f32),
             pltpu.VMEM((stages, members // 2 + 8, members), f32),
             dma((chunks,)), dma((chunks,)), dma((fields * rows,)),

time: 101 us -> 97.3 us (0.963)
  Pallas kernels: 101 us -> 97.1 us
    pallas_call x1, Pallas kernels: 88.1 us -> 84.1 us  [shards(): pl.pallas_call(functools.partial(forecast_kernel, n_lat, n_lon), out_shap...]
where the time goes in v6:
time: 97.3 us; the launch traced here: 97.1 us
  Pallas kernels  97.1 us (100%)
    pallas_call x1, Pallas kernels, shards(): pl.pallas_call(functools.partial(forecast_kernel, n_lat, n_lon), out_shap...  84.1 us
    pallas_call x1, Pallas kernels, shards(): pl.pallas_call(analysis_kernel, grid=(fields,), out_shape=jax.ShapeDtypeS...  13 us

profile of v6, /device:TPU:0, one launch (start us, length us, event | category | flops | bytes accessed | tf_op | source)
XLA Modules:
  0.0 97.1 jit_solution(6293304964029588046)
XLA Ops:
  0.0 84.1 %forecast.1 = (bf16[24,256,512]{2,1,0:T(8,128)(2,1)}, f32[24,1,512]{2,1,0:T(1,128)}, f32[72,128]{1,0:T(8,128)}) custom-call(f32[128,3,8,512]{3,2,1,0:T(8,128)} %state_hbm.1, bf16[128,8,512]{2,1,0:T(8,128)(2,1)} %force_hbm.1, s32[1,1,64]{2,1,0:T(1,128)} %index_ref.1, f32[1,1,64]{2,1,0:T(1,128)} %value_ref.1, f32[1,1,64]{2,1,0:T(1,128)} %error_ref.1), custom_call_target="tpu_custom_call" | custom-call | tf_op jit(solution)/shard_map/forecast/pallas_call | solution.py:400
  84.1 13.0 %analysis.1 = f32[128,3,8,512]{3,2,1,0:T(8,128)} custom-call(f32[72,128]{1,0:T(8,128)} %get-tuple-element.8.sums_ref, bf16[24,256,512]{2,1,0:T(8,128)(2,1)} %get-tuple-element.9.terms_ref, f32[24,1,512]{2,1,0:T(1,128)} %get-tuple-element.10.mean_ref), custom_call_target="tpu_custom_call" | custom-call | tf_op jit(solution)/shard_map/analysis/pallas_call | solution.py:428

commit v7 on v6

--- a/solution.py
+++ b/solution.py
@@ -72,8 +72,8 @@
 
 
 def forecast_kernel(n_lat, n_lon, state_hbm, force_hbm, index_ref, value_ref, error_ref, terms_hbm, mean_ref, sums_ref,
-                    raw, force, ext, relay, cols_out, cols_in, fore, terms, onehot, acc, acc_in,
-                    in_sem, force_sem, out_sem, row_send, row_recv, relay_recv, relay_send, col_send, col_recv, sum_send, sum_recv):
+                    raw, force, ext, relay, cols_out, cols_in, fore, terms, onehot, readings, acc, acc_in, part, part_in, whole,
+                    in_sem, force_sem, out_sem, row_send, row_recv, relay_recv, relay_send, col_send, col_recv, sum_send, sum_recv, cut_send, cut_recv, join_send, join_recv):
     chunks = raw.shape[0]
     members = chunks * CHUNK
     sites = index_ref.shape[-1]
@@ -96,8 +96,8 @@
     def dev(place):
         return {"lat": place[0], "lon": place[1]}
 
-    partners = [(lat, lon ^ d) for d in doublings(n_lon)] + [(lat ^ d, lon) for d in doublings(n_lat)]
-    far = [(lat, lon ^ d) for d in doublings(n_lon)[1:]] + [(lat ^ d, lon) for d in doublings(n_lat)[1:]]
+    far = ([(lat, lax.rem(lon + d, n_lon)) for d in range(1, n_lon)]
+           + [(lat ^ d, lon) for d in doublings(n_lat)[1:]])
 
     def load(c):
         return pltpu.make_async_copy(state_hbm.at[pl.ds(c * CHUNK, CHUNK)], raw.at[c], in_sem.at[c])
@@ -111,7 +111,7 @@
         load_force(c).start()
 
     barrier = pltpu.get_barrier_semaphore()
-    for place in [east, west] + far:
+    for place in far:
         pl.semaphore_signal(barrier, inc=1, device_id=dev(place), device_id_type=MESH)
 
     @pl.when(has_south)
@@ -149,7 +149,7 @@
                 ext[step, c, :, rows + 1] = jnp.zeros((3, CHUNK, width), jnp.float32)
 
     present = [has_south, has_north, lat > 1, lat < n_lat - 2]
-    pl.semaphore_wait(barrier, 2 + len(far) + sum(there.astype(jnp.int32) for there in present))
+    pl.semaphore_wait(barrier, len(far) + sum(there.astype(jnp.int32) for there in present))
 
     def row_copy(step, c, side):
         return pltpu.make_async_remote_copy(
@@ -287,30 +287,51 @@
                 fore[c, f, r] = new[f]
 
         advance(1, c, put)
+        seen = jnp.zeros((CHUNK, sites), jnp.float32)
+        for r in range(rows):
+            picked = jnp.dot(jnp.concatenate(parts_of(fore[c, 0, r], 3), axis=0), onehot[r],
+                             preferred_element_type=jnp.float32)
+            seen += (picked[:CHUNK] + picked[CHUNK:2 * CHUNK]) + picked[2 * CHUNK:]
+        readings[c] = seen
 
     pl.loop(0, chunks)(begin)
     pl.loop(0, chunks)(first_step)
     pl.loop(0, chunks)(second_step)
 
-    seen = jnp.zeros((members, sites), jnp.float32)
-    for r in range(rows):
-        terms_here = parts_of(fore[:, 0, r].reshape(members, width), 3)
-        picked = jnp.dot(jnp.concatenate(terms_here, axis=0), onehot[r], preferred_element_type=jnp.float32)
-        seen += (picked[:members] + picked[members:2 * members]) + picked[2 * members:]
+    seen = readings[...].reshape(members, sites)
     mean = jnp.mean(seen, axis=0, keepdims=True)
     spread = seen - mean
     inv = 1.0 / error_ref[0]
     innovation = inv * (value_ref[0] - mean)
     left = jnp.concatenate([spread * inv, jnp.broadcast_to(innovation, (8, sites))], axis=0)
-    acc[0] = fold(product(left, spread.T))
+    folded = fold(product(left, spread.T))
+    acc[:folded.shape[0]] = folded
+    acc[folded.shape[0]:] = jnp.zeros((acc.shape[0] - folded.shape[0], members), jnp.float32)
+    piece = part.shape[1]
+
+    def rows_of(place):
+        return pl.ds(pl.multiple_of(place * piece, 8), piece)
+
+    def cut_copy(d):
+        place = lax.rem(lon + d, n_lon)
+        return pltpu.make_async_remote_copy(
+            src_ref=acc.at[rows_of(place)], dst_ref=acc_in.at[d - 1], send_sem=cut_send.at[d - 1],
+            recv_sem=cut_recv.at[d - 1], device_id=dev((lat, place)), device_id_type=MESH)
+
+    def join_copy(d):
+        return pltpu.make_async_remote_copy(
+            src_ref=whole.at[rows_of(lon)], dst_ref=whole.at[rows_of(lon)], send_sem=join_send.at[d - 1],
+            recv_sem=join_recv.at[d - 1], device_id=dev((lat, lax.rem(lon + d, n_lon))), device_id_type=MESH)
+
     swaps = [pltpu.make_async_remote_copy(
-        src_ref=acc.at[s], dst_ref=acc_in.at[s], send_sem=sum_send.at[s], recv_sem=sum_recv.at[s],
-        device_id=dev(place), device_id_type=MESH) for s, place in enumerate(partners)]
+        src_ref=part.at[s], dst_ref=part_in.at[s], send_sem=sum_send.at[s], recv_sem=sum_recv.at[s],
+        device_id=dev((lat ^ d, lon)), device_id_type=MESH) for s, d in enumerate(doublings(n_lat))]
+    others = range(1, n_lon)
     items = 3 * rows
-    for s, swap in enumerate(swaps):
-        swap.start()
-
-        @pl.loop(s * items // len(swaps), (s + 1) * items // len(swaps))
+    slots = len(swaps) + 2
+
+    def split_terms(slot):
+        @pl.loop(slot * items // slots, (slot + 1) * items // slots)
         def _(i):
             cells = fore[:, i // rows, lax.rem(i, rows)].reshape(members, width)
             mean = jnp.mean(cells, axis=0, keepdims=True)
@@ -318,9 +339,29 @@
             mean_ref[i] = mean
             save(i).start()
 
+    for d in others:
+        cut_copy(d).start()
+    split_terms(0)
+    total = acc[rows_of(lon)]
+    for d in others:
+        cut_copy(d).wait_recv()
+        total += acc_in[d - 1]
+    part[0] = total
+    for s, swap in enumerate(swaps):
+        swap.start()
+        split_terms(s + 1)
         swap.wait_recv()
-        acc[s + 1] = acc[s] + acc_in[s]
-    sums_ref[...] = acc[len(swaps)]
+        part[s + 1] = part[s] + part_in[s]
+    whole[rows_of(lon)] = part[len(swaps)]
+    for d in others:
+        join_copy(d).start()
+    split_terms(slots - 1)
+    for d in others:
+        join_copy(d).wait_recv()
+    sums_ref[...] = whole[:sums_ref.shape[0]]
+    for d in others:
+        cut_copy(d).wait_send()
+        join_copy(d).wait_send()
     for swap in swaps:
         swap.wait_send()
 
@@ -352,7 +393,7 @@
     half = members // 2
     rows = terms_ref.shape[0]
 
-    @pl.when(pl.program_id(0) == 0)
+    @pl.when((pl.program_id(0) == 0) & (pl.program_id(1) == 0))
     def _():
         eye = (lax.broadcasted_iota(jnp.int32, (members, members), 0)
                == lax.broadcasted_iota(jnp.int32, (members, members), 1)).astype(jnp.float32)
@@ -393,7 +434,8 @@
     sites = obs_index.shape[-1]
     vmem = pl.BlockSpec(memory_space=pltpu.VMEM)
     anywhere = pl.BlockSpec(memory_space=pl.ANY)
-    stages = len(doublings(n_lon)) + len(doublings(n_lat))
+    stages = len(doublings(n_lat))
+    piece = 8 * -(-(members // 2 + 8) // (8 * n_lon))
     dma = pltpu.SemaphoreType.DMA
     f32 = jnp.float32
     block = (chunks, fields, rows, CHUNK, width)
@@ -414,27 +456,32 @@
             pltpu.VMEM(block, f32),
             pltpu.VMEM((fields * rows, 2 * members, width), jnp.bfloat16),
             pltpu.VMEM((rows, width, sites), jnp.bfloat16),
-            pltpu.VMEM((stages + 1, members // 2 + 8, members), f32),
-            pltpu.VMEM((stages, members // 2 + 8, members), f32),
+            pltpu.VMEM((chunks, CHUNK, sites), f32),
+            pltpu.VMEM((piece * n_lon, members), f32),
+            pltpu.VMEM((n_lon - 1, piece, members), f32),
+            pltpu.VMEM((stages + 1, piece, members), f32),
+            pltpu.VMEM((stages, piece, members), f32),
+            pltpu.VMEM((piece * n_lon, members), f32),
             dma((chunks,)), dma((chunks,)), dma((fields * rows,)),
             dma((2, 2, chunks)), dma((2, 2, chunks)),
             dma((2, chunks)), dma((2, chunks)),
             dma((2, 2, chunks)), dma((2, 2, chunks)),
             dma((stages,)), dma((stages,)),
+            dma((n_lon - 1,)), dma((n_lon - 1,)), dma((n_lon - 1,)), dma((n_lon - 1,)),
         ],
         compiler_params=pltpu.CompilerParams(collective_id=0, has_side_effects=True, vmem_limit_bytes=63 << 20),
         name="forecast",
     )(ocean_status, height_driver, obs_index, obs_value, obs_error)
     return pl.pallas_call(
         analysis_kernel,
-        grid=(fields,),
+        grid=(fields, 2),
         out_shape=jax.ShapeDtypeStruct(ocean_status.shape, f32),
-        in_specs=[pl.BlockSpec((members // 2 + 8, members), lambda i: (0, 0)),
-                  pl.BlockSpec((rows, 2 * members, width), lambda i: (i, 0, 0)),
-                  pl.BlockSpec((rows, 1, width), lambda i: (i, 0, 0))],
-        out_specs=pl.BlockSpec((members, 1, rows, width), lambda i: (0, i, 0, 0)),
+        in_specs=[pl.BlockSpec((members // 2 + 8, members), lambda i, j: (0, 0)),
+                  pl.BlockSpec((rows, 2 * members, width // 2), lambda i, j: (i, 0, j)),
+                  pl.BlockSpec((rows, 1, width // 2), lambda i, j: (i, 0, j))],
+        out_specs=pl.BlockSpec((members, 1, rows, width // 2), lambda i, j: (0, i, 0, j)),
         scratch_shapes=[pltpu.VMEM((2 * members, 2 * members), jnp.bfloat16),
-                        pltpu.VMEM((rows, members, width), f32)],
+                        pltpu.VMEM((rows, members, width // 2), f32)],
         compiler_params=pltpu.CompilerParams(vmem_limit_bytes=63 << 20),
         name="analysis",
     )(sums, terms, mean)

time: 97.3 us -> 97.9 us (level)
  no operation moved by 1% of the time
where the time goes in v7:
time: 97.9 us; the launch traced here: 97.7 us
  Pallas kernels  97.6 us (100%)
    pallas_call x1, Pallas kernels, shards(): pl.pallas_call(functools.partial(forecast_kernel, n_lat, n_lon), out_shap...  84.6 us
    pallas_call x1, Pallas kernels, shards(): pl.pallas_call(analysis_kernel, grid=(fields, 2), out_shape=jax.ShapeDtyp...  13.1 us

profile of v7, /device:TPU:0, one launch (start us, length us, event | category | flops | bytes accessed | tf_op | source)
XLA Modules:
  0.0 97.7 jit_solution(8499355003935962580)
XLA Ops:
  0.0 84.6 %forecast.1 = (bf16[24,256,512]{2,1,0:T(8,128)(2,1)}, f32[24,1,512]{2,1,0:T(1,128)}, f32[72,128]{1,0:T(8,128)}) custom-call(f32[128,3,8,512]{3,2,1,0:T(8,128)} %state_hbm.1, bf16[128,8,512]{2,1,0:T(8,128)(2,1)} %force_hbm.1, s32[1,1,64]{2,1,0:T(1,128)} %index_ref.1, f32[1,1,64]{2,1,0:T(1,128)} %value_ref.1, f32[1,1,64]{2,1,0:T(1,128)} %error_ref.1), custom_call_target="tpu_custom_call" | custom-call | tf_op jit(solution)/shard_map/forecast/pallas_call | solution.py:442
  84.6 13.1 %analysis.1 = f32[128,3,8,512]{3,2,1,0:T(8,128)} custom-call(f32[72,128]{1,0:T(8,128)} %get-tuple-element.8.sums_ref, bf16[24,256,512]{2,1,0:T(8,128)(2,1)} %get-tuple-element.9.terms_ref, f32[24,1,512]{2,1,0:T(1,128)} %get-tuple-element.10.mean_ref), custom_call_target="tpu_custom_call" | custom-call | tf_op jit(solution)/shard_map/analysis/pallas_call | solution.py:475

commit v8 on v4

--- a/solution.py
+++ b/solution.py
@@ -108,6 +108,9 @@
     @pl.loop(0, chunks)
     def _(c):
         load(c).start()
+
+    @pl.loop(0, chunks)
+    def _(c):
         load_force(c).start()
 
     barrier = pltpu.get_barrier_semaphore()
@@ -359,14 +362,13 @@
         def turn(_, pair):
             upper, lower = pair
             factor = 1.5 * eye - 0.5 * paired(lower, upper)
-            both = paired(jnp.concatenate([upper, lower], axis=0), factor)
-            return both[:members], both[members:]
+            return paired(factor, upper), paired(factor, lower)
 
         upper = amat / scale
         lower = 1.5 * eye - 0.5 * upper
-        upper = paired(upper, lower)
-        upper, lower = lax.fori_loop(1, NS_ITERS - 1, turn, (upper, lower))
-        lower = paired(lower, 1.5 * eye - 0.5 * paired(lower, upper))
+        upper = paired(lower, upper)
+        upper, lower = lax.fori_loop(1, NS_ITERS - 1, turn, (upper, lower), unroll=True)
+        lower = paired(1.5 * eye - 0.5 * paired(lower, upper), lower)
         root = lower / jnp.sqrt(scale)
         inverse = paired(root, root)
         shift = paired(sums_ref[half:], inverse.T)

time: 97.4 us -> 96.4 us (0.990)
  Pallas kernels: 97.2 us -> 96.2 us
where the time goes in v8:
time: 96.4 us; the launch traced here: 96.2 us
  Pallas kernels  96.2 us (100%)
    pallas_call x1, Pallas kernels, shards(): pl.pallas_call(functools.partial(forecast_kernel, n_lat, n_lon), out_shap...  83.3 us
    pallas_call x1, Pallas kernels, shards(): pl.pallas_call(analysis_kernel, grid=(fields,), out_shape=jax.ShapeDtypeS...  13 us

profile of v8, /device:TPU:0, one launch (start us, length us, event | category | flops | bytes accessed | tf_op | source)
XLA Modules:
  0.0 96.2 jit_solution(15417401975601130852)
XLA Ops:
  0.0 83.3 %forecast.1 = (bf16[24,256,512]{2,1,0:T(8,128)(2,1)}, f32[24,1,512]{2,1,0:T(1,128)}, f32[72,128]{1,0:T(8,128)}) custom-call(f32[128,3,8,512]{3,2,1,0:T(8,128)} %state_hbm.1, bf16[128,8,512]{2,1,0:T(8,128)(2,1)} %force_hbm.1, s32[1,1,64]{2,1,0:T(1,128)} %index_ref.1, f32[1,1,64]{2,1,0:T(1,128)} %value_ref.1, f32[1,1,64]{2,1,0:T(1,128)} %error_ref.1), custom_call_target="tpu_custom_call" | custom-call | tf_op jit(solution)/shard_map/forecast/pallas_call | solution.py:400
  83.3 13.0 %analysis.1 = f32[128,3,8,512]{3,2,1,0:T(8,128)} custom-call(f32[72,128]{1,0:T(8,128)} %get-tuple-element.8.sums_ref, bf16[24,256,512]{2,1,0:T(8,128)(2,1)} %get-tuple-element.9.terms_ref, f32[24,1,512]{2,1,0:T(1,128)} %get-tuple-element.10.mean_ref), custom_call_target="tpu_custom_call" | custom-call | tf_op jit(solution)/shard_map/analysis/pallas_call | solution.py:429
